TPU v7x, 32 devices: a whole 2x2x4 slice. The times are simulated.
32 devices in a mesh: row: 4 (over y, x), col: 8 (over z, core).
Axes of the slice: x: 2, y: 2, z: 4, core: 2. Of those that a mesh axis runs over, the one named last changes fastest.
Arguments:
- amplitudes: float32 [8, 8, 256, 256], P('row', 'col'), may hold values from -6 to 6
- coulomb: bfloat16 [8, 8, 256, 256], P('row'), may hold values from -6 to 6
- inner_list: int32 [8, 8, 8], P('row', 'col'), may hold values from 0 to 7, as said below
- inner_count: int32 [8, 8], P('row', 'col'), may hold values from 4 to 8
- reader_list: int32 [8, 8, 8], P('row'), may hold values from 0 to 7, as said below
- reader_count: int32 [8, 8], P('row'), may hold values from 4 to 8
- virtual_energy: float32 [256], replicated, may hold values from 0.5 to 2.5
- occupied_energy: float32 [8], replicated, may hold values from -1.5 to -0.3
Outputs:
- new_amplitudes: float32 [8, 8, 256, 256], P('row', 'col')
Inputs may be any that keep to these rules, and one draw needn't show every extreme that they name: `inner_list`: for each pair block the 8 entries are distinct orbitals; only the first inner_count of them are used. `reader_list`: for each pair block the 8 entries are distinct orbitals; only the first reader_count of them are used.
All inputs are finite; a program needn't handle non-finite values.
Results may differ from a plain program's by a relative error of at most 0.0015.
Values may be sent and summed in bfloat16 or wider, within the bound.
No kernel may reach another device: no remote copies, remote signals or barrier semaphores. Data moves between devices by JAX's collectives and lax.ppermute only.
A program may use at most 64 MiB of HBM per device.

v0:
```python
import jax
import jax.numpy as jnp
from jax import lax
from jax.sharding import PartitionSpec as P

ITERS = 2


damping = 0.5
coupling = 0.03125


def on_device(
    amplitudes,
    coulomb,
    inner_list,
    inner_count,
    reader_list,
    reader_count,
    virtual_energy,
    occupied_energy,
):
    orb_rows = amplitudes.shape[0]
    orb_cols = amplitudes.shape[1]
    slot_count = inner_list.shape[2]
    row_start = lax.axis_index("row") * orb_rows
    col_start = lax.axis_index("col") * orb_cols
    occ_rows = lax.dynamic_slice_in_dim(occupied_energy, row_start, orb_rows, 0)
    occ_cols = lax.dynamic_slice_in_dim(occupied_energy, col_start, orb_cols, 0)
    virt_pair = virtual_energy[:, None] + virtual_energy[None, :]
    denominator = (
        virt_pair[None, None] - occ_rows[:, None, None, None] - occ_cols[None, :, None, None]
    )
    slot_iota = jnp.arange(slot_count, dtype=jnp.int32)
    row_iota = jnp.arange(orb_rows, dtype=jnp.int32)[:, None, None]
    col_iota = jnp.arange(orb_cols, dtype=jnp.int32)[None, :, None]
    inner_mask = (slot_iota < inner_count[..., None]).astype(jnp.bfloat16)[..., None, None]
    own_readers = lax.dynamic_slice_in_dim(reader_list, col_start, orb_cols, 1)
    own_reader_len = lax.dynamic_slice_in_dim(reader_count, col_start, orb_cols, 1)
    reader_mask = (slot_iota < own_reader_len[..., None]).astype(jnp.bfloat16)[..., None, None]
    coulomb_own = lax.dynamic_slice_in_dim(coulomb, col_start, orb_cols, 1).astype(jnp.float32)
    left_inner = coulomb[row_iota, inner_list]
    amp_state = amplitudes
    for sweep_index in range(ITERS):
        amp_half = amp_state.astype(jnp.bfloat16)
        amp_columns = lax.all_gather(amp_half, "row", axis=0, tiled=True)
        right_inner = amp_columns[inner_list, col_iota] * inner_mask
        coupled = jnp.einsum(
            "ijsab,ijsbc->ijac", left_inner, right_inner, preferred_element_type=jnp.float32
        ).astype(jnp.bfloat16)
        coupled_columns = lax.all_gather(coupled, "row", axis=0, tiled=True)
        coupled_rows = lax.all_to_all(
            coupled_columns, "col", split_axis=0, concat_axis=1, tiled=True
        )
        mirror = jnp.transpose(
            lax.dynamic_slice_in_dim(coupled_rows, row_start, orb_rows, 1), (1, 0, 3, 2)
        )
        right_reader = coupled_columns[own_readers, col_iota] * reader_mask
        amp_rows = lax.all_gather(amp_half, "col", axis=1, tiled=True)
        left_reader = amp_rows[row_iota, own_readers]
        quadratic = jnp.einsum(
            "ijsab,ijsbc->ijac", left_reader, right_reader, preferred_element_type=jnp.float32
        )
        residual = (
            coulomb_own
            + coupling * (coupled.astype(jnp.float32) + mirror.astype(jnp.float32))
            + coupling * coupling * quadratic
        )
        amp_state = damping * amp_state - residual / denominator
    return amp_state


def solution(mesh):
    return jax.shard_map(
        on_device,
        mesh=mesh,
        in_specs=(
            P("row", "col", None, None),
            P("row", None, None, None),
            P("row", "col", None),
            P("row", "col"),
            P("row", None, None),
            P("row", None),
            P(),
            P(),
        ),
        out_specs=P("row", "col", None, None),
        check_vma=False,
    )
```

profile of v0, /device:TPU:7, one launch (start us, length us, event | category | flops | bytes accessed | tf_op | source)
XLA Modules:
  0.0 252.2 jit_solution(13133688176738046651)
XLA Ops:
  6.5 1.8 convert_element_type.66
  8.4 0.7 compare_select_fusion
  9.1 0.1 reshape.174
  9.4 2.3 gather_fusion
  11.7 24.4 %all-gather.9.cloned.1.call-done = bf16[8,1,256,256]{3,2,1,0:T(8,128)(2,1)} async-done(((bf16[2,1,256,256]{3,2,1,0:T(8,128)(2,1)}), bf16[8,1,256,256]{3,2,1,0:T(8,128)(2,1)}) %all-gather.9.cloned.1.call-update) | async-done | bytes 1048592 | tf_op jit(solution)/shard_map/all_gather | solution.py:46
  36.1 3.2 %gather_fusion.1 = bf16[16,256,256]{2,1,0:T(8,128)(2,1)} fusion(bf16[8,1,256,256]{3,2,1,0:T(8,128)(2,1)} %all-gather.9.cloned.1.call-done, s32[16]{0:T(128)S(1)} %reshape.174), kind=kCustom, calls=%fused_computation.1 | custom fusion | bytes 4194432 | tf_op jit(solution)/shard_map/gather | solution.py:47
  39.4 3.1 %fusion.41 = bf16[2,256,256]{2,1,0:T(8,128)(2,1)} fusion(bf16[2,8,256,256]{3,2,1,0:T(8,128)(2,1)S(1)} %bitcast.133, bf16[2,8,256,256]{3,2,1,0:T(8,128)(2,1)} %bitcast.140, bf16[2,8]{1,0:T(2,128)(2,1)S(1)} %compare_convert_fusion.1), kind=kOutput, calls=%fused_computation.26 | convolution fusion | flops 538050560 | bytes 4456480 | tf_op jit(solution)/shard_map/ijsab,ijsbc->ijac/dot_general | solution.py:48
  42.6 0.7 all-gather.11.cloned.1.call-update
  43.2 26.0 %all-gather.17.cloned.1.call-done = bf16[8,256,256]{2,1,0:T(8,128)(2,1)} async-done(((bf16[2,256,256]{2,1,0:T(8,128)(2,1)}), bf16[8,256,256]{2,1,0:T(8,128)(2,1)}) %all-gather.17.cloned.1.call-update) | async-done | bytes 1048592 | tf_op jit(solution)/shard_map/all_gather | solution.py:51
  69.3 5.4 %all-to-all-start = ((bf16[8,1,256,256]{3,2,1,0:T(8,128)(2,1)}), bf16[8,1,256,256]{3,2,1,0:T(8,128)(2,1)}, u32[]{:S(2)}, u32[]{:S(2)}) async-start(bf16[8,1,256,256]{3,2,1,0:T(8,128)(2,1)} %bitcast.129), calls=%async_computation | async-start | bytes 2097152 | tf_op jit(solution)/shard_map/all_to_all | solution.py:52
  74.7 0.6 dynamic_slice.21
  75.4 0.2 fusion.67
  75.6 0.1 reshape.190
  75.9 0.1 broadcast_add_fusion
  76.0 2.0 gather_fusion.3
  78.0 41.4 %all-gather.11.cloned.1.call-done = bf16[2,8,256,256]{3,2,1,0:T(8,128)(2,1)} async-done(((bf16[2,1,256,256]{3,2,1,0:T(8,128)(2,1)}), bf16[2,8,256,256]{3,2,1,0:T(8,128)(2,1)}) %all-gather.11.cloned.1.call-update) | async-done | bytes 2097168 | tf_op jit(solution)/shard_map/all_gather | solution.py:59
  119.4 3.6 %gather_fusion.2 = bf16[16,256,256]{2,1,0:T(8,128)(2,1)} fusion(bf16[2,8,256,256]{3,2,1,0:T(8,128)(2,1)} %all-gather.11.cloned.1.call-done, s32[16]{0:T(128)S(1)} %reshape.182), kind=kCustom, calls=%fused_computation.2 | custom fusion | bytes 4194432 | tf_op jit(solution)/shard_map/gather | solution.py:60
  123.0 1.0 constant_dynamic-slice_fusion.3
  124.0 0.8 copy.39
  124.9 4.7 %fusion.84 = (bf16[2,1,256,256]{3,2,0,1:T(8,128)(2,1)}, f32[2,1,256,256]{3,2,0,1:T(8,128)}) fusion(f32[]{:T(128)} %bitcast.22, f32[2]{0:T(128)S(1)} %dynamic_slice.20, f32[256,256]{1,0:T(8,128)S(1)} %broadcast_add_fusion, bf16[2,8,256,256]{3,2,1,0:T(8,128)(2,1)} %bitcast.138, bf16[2,8,256,256]{3,2,1,0:T(8,128)(2,1)} %bitcast.137, ...), kind=kOutput, calls=%fused_computation.86 | convolution fusion | flops 539754496 | bytes 6553648 | tf_op jit(solution)/shard_map/ijsab,ijsbc->ijac/dot_general | solution.py:61
  129.7 23.6 %all-gather.13.cloned.1.call-done = bf16[8,1,256,256]{3,2,1,0:T(8,128)(2,1)} async-done(((bf16[2,1,256,256]{3,2,1,0:T(8,128)(2,1)}), bf16[8,1,256,256]{3,2,1,0:T(8,128)(2,1)}) %all-gather.13.cloned.1.call-update) | async-done | bytes 1048592 | tf_op jit(solution)/shard_map/all_gather | solution.py:46
  153.2 3.2 %gather_fusion.4 = bf16[16,256,256]{2,1,0:T(8,128)(2,1)} fusion(bf16[8,1,256,256]{3,2,1,0:T(8,128)(2,1)} %all-gather.13.cloned.1.call-done, s32[16]{0:T(128)S(1)} %reshape.174), kind=kCustom, calls=%fused_computation.4 | custom fusion | bytes 4194432 | tf_op jit(solution)/shard_map/gather | solution.py:47
  156.5 3.1 %fusion.38 = bf16[2,256,256]{2,1,0:T(8,128)(2,1)} fusion(bf16[2,8,256,256]{3,2,1,0:T(8,128)(2,1)S(1)} %bitcast.134, bf16[2,8,256,256]{3,2,1,0:T(8,128)(2,1)} %bitcast.139, bf16[2,8]{1,0:T(2,128)(2,1)S(1)} %compare_convert_fusion.1), kind=kOutput, calls=%fused_computation.25 | convolution fusion | flops 538050560 | bytes 4456480 | tf_op jit(solution)/shard_map/ijsab,ijsbc->ijac/dot_general | solution.py:48
  159.7 0.5 all-gather.15.cloned.1.call-update
  160.2 26.2 %all-gather.19.cloned.1.call-done = bf16[8,256,256]{2,1,0:T(8,128)(2,1)} async-done(((bf16[2,256,256]{2,1,0:T(8,128)(2,1)}), bf16[8,256,256]{2,1,0:T(8,128)(2,1)}) %all-gather.19.cloned.1.call-update) | async-done | bytes 1048592 | tf_op jit(solution)/shard_map/all_gather | solution.py:51
  186.4 5.4 %all-to-all-start.1 = ((bf16[8,1,256,256]{3,2,1,0:T(8,128)(2,1)}), bf16[8,1,256,256]{3,2,1,0:T(8,128)(2,1)}, u32[]{:S(2)}, u32[]{:S(2)}) async-start(bf16[8,1,256,256]{3,2,1,0:T(8,128)(2,1)} %bitcast.131), calls=%async_computation.1 | async-start | bytes 2097152 | tf_op jit(solution)/shard_map/all_to_all | solution.py:52
  191.8 0.7 gather_fusion.6
  192.5 44.0 %all-gather.15.cloned.1.call-done = bf16[2,8,256,256]{3,2,0,1:T(8,128)(2,1)} async-done(((bf16[2,1,256,256]{3,2,0,1:T(8,128)(2,1)}), bf16[2,8,256,256]{3,2,0,1:T(8,128)(2,1)}) %all-gather.15.cloned.1.call-update) | async-done | bytes 2097168 | tf_op jit(solution)/shard_map/all_gather | solution.py:59
  236.5 3.6 %gather_fusion.5 = bf16[16,256,256]{2,1,0:T(8,128)(2,1)} fusion(bf16[2,8,256,256]{3,2,0,1:T(8,128)(2,1)} %all-gather.15.cloned.1.call-done, s32[16]{0:T(128)S(1)} %reshape.182), kind=kCustom, calls=%fused_computation.5 | custom fusion | bytes 4194432 | tf_op jit(solution)/shard_map/gather | solution.py:60
  240.1 1.0 constant_dynamic-slice_fusion
  241.1 0.1 copy.40
  241.2 4.1 %fusion.52 = f32[2,1,256,256]{3,2,1,0:T(8,128)} fusion(bf16[2,8,256,256]{3,2,1,0:T(8,128)(2,1)} %bitcast.136, bf16[2,8,256,256]{3,2,1,0:T(8,128)(2,1)S(1)} %bitcast.135, bf16[2,8]{1,0:T(2,128)(2,1)S(1)} %compare_convert_fusion, f32[2,1,256,256]{3,2,0,1:T(8,128)} %get-tuple-element.8, bf16[2,1,256,256]{2,3,0,1:T(8,128)(2,1)S(1)} %copy.40, ...), kind=kOutput, calls=%fused_computation.31 | convolution fusion | flops 539623424 | bytes 6291504 | tf_op jit(solution)/shard_map/ijsab,ijsbc->ijac/dot_general | solution.py:61
  (45 shorter events, 0.8 us)
Async XLA Ops:
  6.5 68.9 %copy-start = (s32[2,8]{1,0:T(2,128)S(1)}, s32[2,8]{1,0:T(2,128)}, u32[]{:S(2)}) copy-start(s32[2,8]{1,0:T(2,128)} %param.13) | copy-start | bytes 196
  6.5 29.6 %all-gather.9.cloned.1.call-start = ((), (), s32[]{:S(2)}) async-start(), calls=%async_computation.2 | async-start | bytes 1310720 | tf_op jit(solution)/shard_map/all_gather | solution.py:46
  8.3 60.9 %all-gather.17.cloned.1.call-start = ((), (), s32[]{:S(2)}) async-start(), calls=%async_computation.6 | async-start | bytes 1310720 | tf_op jit(solution)/shard_map/all_gather | solution.py:51
  9.4 2.3 copy-start.7
  42.5 32.2 %copy-start.8 = (f32[8]{0:T(128)S(1)}, f32[8]{0:T(128)}, u32[]{:S(2)}) copy-start(f32[8]{0:T(128)} %param.15) | copy-start | bytes 100
  42.5 33.4 %copy-start.6 = (f32[256]{0:T(256)S(1)}, f32[256]{0:T(256)}, u32[]{:S(2)}) copy-start(f32[256]{0:T(256)} %param.14) | copy-start | bytes 3076
  42.5 76.9 %all-gather.11.cloned.1.call-start = ((), (), s32[]{:S(2)}) async-start(), calls=%async_computation.3 | async-start | bytes 2359296 | tf_op jit(solution)/shard_map/all_gather | solution.py:59
  69.3 6.7 %copy-start.1 = (bf16[8,256,256]{2,1,0:T(8,128)(2,1)S(1)}, bf16[8,256,256]{2,1,0:T(8,128)(2,1)}, u32[]{:S(2)}) copy-start(bf16[8,256,256]{2,1,0:T(8,128)(2,1)} %all-gather.17.cloned.1.call-done) | copy-start | bytes 3145732
  69.3 53.7 %all-to-all-start = ((bf16[8,1,256,256]{3,2,1,0:T(8,128)(2,1)}), bf16[8,1,256,256]{3,2,1,0:T(8,128)(2,1)}, u32[]{:S(2)}, u32[]{:S(2)}) async-start(bf16[8,1,256,256]{3,2,1,0:T(8,128)(2,1)} %bitcast.129), calls=%async_computation | async-start | bytes 2097152 | tf_op jit(solution)/shard_map/all_to_all | solution.py:52
  74.7 78.5 %all-gather.13.cloned.1.call-start = ((), (), s32[]{:S(2)}) async-start(), calls=%async_computation.4 | async-start | bytes 1310720 | tf_op jit(solution)/shard_map/all_gather | solution.py:46
  78.0 46.9 %copy-start.3 = (f32[2,1,256,256]{3,2,1,0:T(8,128)S(1)}, f32[2,1,256,256]{3,2,1,0:T(8,128)}, u32[]{:S(2)}) copy-start(f32[2,1,256,256]{3,2,1,0:T(8,128)} %param.8) | copy-start | bytes 1572868
  78.0 46.9 %copy-start.4 = (bf16[2,256,256]{2,1,0:T(8,128)(2,1)S(1)}, bf16[2,256,256]{2,1,0:T(8,128)(2,1)}, u32[]{:S(2)}) copy-start(bf16[2,256,256]{2,1,0:T(8,128)(2,1)} %fusion.41) | copy-start | bytes 786436
  129.6 56.8 %all-gather.19.cloned.1.call-start = ((), (), s32[]{:S(2)}) async-start(), calls=%async_computation.7 | async-start | bytes 1310720 | tf_op jit(solution)/shard_map/all_gather | solution.py:51
  159.6 76.9 %all-gather.15.cloned.1.call-start = ((), (), s32[]{:S(2)}) async-start(), calls=%async_computation.5 | async-start | bytes 2359296 | tf_op jit(solution)/shard_map/all_gather | solution.py:59
  186.4 5.4 %copy-start.2 = (bf16[8,256,256]{2,1,0:T(8,128)(2,1)S(1)}, bf16[8,256,256]{2,1,0:T(8,128)(2,1)}, u32[]{:S(2)}) copy-start(bf16[8,256,256]{2,1,0:T(8,128)(2,1)} %all-gather.19.cloned.1.call-done) | copy-start | bytes 3145732
  186.4 53.7 %all-to-all-start.1 = ((bf16[8,1,256,256]{3,2,1,0:T(8,128)(2,1)}), bf16[8,1,256,256]{3,2,1,0:T(8,128)(2,1)}, u32[]{:S(2)}, u32[]{:S(2)}) async-start(bf16[8,1,256,256]{3,2,1,0:T(8,128)(2,1)} %bitcast.131), calls=%async_computation.1 | async-start | bytes 2097152 | tf_op jit(solution)/shard_map/all_to_all | solution.py:52
  192.5 48.7 %copy-start.5 = (bf16[2,256,256]{2,1,0:T(8,128)(2,1)S(1)}, bf16[2,256,256]{2,1,0:T(8,128)(2,1)}, u32[]{:S(2)}) copy-start(bf16[2,256,256]{2,1,0:T(8,128)(2,1)} %fusion.38) | copy-start | bytes 786436
Sparse Core Ops, SparseCore 0:
  9.2 26.8 all-gather.8
  42.6 26.6 all-gather.16
  70.9 48.4 all-gather.10
  129.7 23.4 all-gather.12
  159.7 26.6 all-gather.18
  187.8 48.5 all-gather.14
where the time goes:
time: 255 us; the launch traced here: 252 us
  waiting for transfers between devices  187 us (73%)
  local copies, waits for them, and re-layouts  22.9 us (9%)
  matrix products  15 us (6%)
  between operations  13.6 us (5%)
  starting transfers between devices  11 us (4%)
  other arithmetic  2.85 us (1%)
    all_gather x2, waiting for transfers between devices, on_device(): amp_rows = lax.all_gather(amp_half, 'col', axis=1, tiled=True)  85.4 us
    all_gather x2, waiting for transfers between devices, on_device(): coupled_columns = lax.all_gather(coupled, 'row', axis=0, tiled=True)  52.2 us
    all_gather x2, waiting for transfers between devices, on_device(): amp_columns = lax.all_gather(amp_half, 'row', axis=0, tiled=True)  48 us
    all_to_all x2, starting transfers between devices, on_device(): lax.all_to_all(coupled_columns, 'col', split_axis=0, concat_axis=1, tiled...  10.8 us
    dot_general x2, matrix products, on_device(): jnp.einsum('ijsab,ijsbc->ijac', left_reader, right_reader, preferred_elem...  8.82 us
    gather x2, local copies, waits for them, and re-layouts, on_device(): left_reader = amp_rows[row_iota, own_readers]  7.23 us
    gather x2, local copies, waits for them, and re-layouts, on_device(): right_inner = amp_columns[inner_list, col_iota] * inner_mask  6.49 us
    dot_general x2, matrix products, on_device(): jnp.einsum('ijsab,ijsbc->ijac', left_inner, right_inner, preferred_elemen...  6.2 us
  transfers between devices with their start and end apart: 8, of which 6 were waited for; matrix products, arithmetic and copies ran while one was open for 6% of the time, Pallas kernels for 0%

commit v1 on v0

v1 whole, which is shorter than its diff:
```python
import functools

import jax
import jax.numpy as jnp
from jax import lax
from jax.experimental import pallas as pl
from jax.experimental.pallas import tpu as pltpu
from jax.sharding import PartitionSpec as P

ITERS = 2


damping = 0.5
coupling = 0.03125
ANY = pl.BlockSpec(memory_space=pl.ANY)
SMEM = pl.BlockSpec(memory_space=pltpu.SMEM)
VMEM = pl.BlockSpec(memory_space=pltpu.VMEM)
VMEM_BYTES = 32 * 1024 * 1024


def coupled_body(rows, meta, k_hbm, *refs):
    pieces = refs[:rows]
    out_ref, k_buf, a_buf, acc, k_sem, a_sem = refs[rows:]
    orb_rows = out_ref.shape[0]
    me = meta[2 * orb_rows, 0]
    k_copy = pltpu.make_async_copy(k_hbm, k_buf, k_sem)
    k_copy.start()
    copies = []
    for step in range(rows):
        start = (me ^ step) * orb_rows
        copy = pltpu.make_async_copy(pieces[step], a_buf.at[pl.ds(start, orb_rows)], a_sem.at[step])
        copy.start()
        copies.append(copy)
    acc[...] = jnp.zeros_like(acc)
    k_copy.wait()
    for step in range(rows):
        copies[step].wait()
        for t in range(orb_rows):
            orbital = (me ^ step) * orb_rows + t
            for i in range(orb_rows):

                @pl.when(meta[i, orbital] > 0)
                def _():
                    acc[i] += jnp.dot(k_buf[i, orbital], a_buf[orbital], preferred_element_type=jnp.float32)

    out_ref[...] = acc[...].astype(out_ref.dtype)


def coupled_blocks(rows, meta, coulomb, pieces):
    orb_rows, count, virt, _ = coulomb.shape
    return pl.pallas_call(
        functools.partial(coupled_body, rows),
        out_shape=jax.ShapeDtypeStruct((orb_rows, virt, virt), jnp.bfloat16),
        in_specs=[SMEM, ANY] + [ANY] * rows,
        out_specs=VMEM,
        scratch_shapes=[
            pltpu.VMEM((orb_rows, count, virt, virt), jnp.bfloat16),
            pltpu.VMEM((count, virt, virt), jnp.bfloat16),
            pltpu.VMEM((orb_rows, virt, virt), jnp.float32),
            pltpu.SemaphoreType.DMA,
            pltpu.SemaphoreType.DMA((rows,)),
        ],
        compiler_params=pltpu.CompilerParams(vmem_limit_bytes=VMEM_BYTES),
        cost_estimate=pl.CostEstimate(
            flops=2 * orb_rows * count * virt**3, bytes_accessed=2 * (orb_rows + 1) * count * virt**2, transcendentals=0
        ),
    )(meta, coulomb, *pieces)


def update_body(rows, halves, meta, *refs):
    c_pieces = refs[:rows]
    d_pieces = refs[rows : rows + 2 * halves]
    base_ref, state_ref, denom_ref = refs[rows + 2 * halves : rows + 2 * halves + 3]
    out_ref, half_ref, c_buf, d_buf, acc, c_sem, d_sem = refs[rows + 2 * halves + 3 :]
    orb_rows = out_ref.shape[0]
    me_row = meta[2 * orb_rows, 0]
    me_col = meta[2 * orb_rows, 1]
    copies = []
    for at in range(2 * halves):
        copy = pltpu.make_async_copy(d_pieces[at], d_buf.at[me_col ^ at], d_sem.at[at])
        copy.start()
        copies.append(copy)
    for step in range(rows):
        start = (me_row ^ step) * orb_rows
        copy = pltpu.make_async_copy(c_pieces[step], c_buf.at[pl.ds(start, orb_rows)], c_sem.at[step])
        copy.start()
        copies.append(copy)
    acc[...] = jnp.zeros_like(acc)
    for copy in copies:
        copy.wait()
    for orbital in range(c_buf.shape[0]):
        for i in range(orb_rows):

            @pl.when(meta[orb_rows + i, orbital] > 0)
            def _():
                acc[i] += jnp.dot(d_buf[orbital, i], c_buf[orbital], preferred_element_type=jnp.float32)

    residual = base_ref[...] + coupling * coupling * acc[...]
    state = damping * state_ref[...] - residual / denom_ref[...]
    out_ref[...] = state
    half_ref[...] = state.astype(half_ref.dtype)


def updated_state(rows, halves, meta, c_pieces, d_pieces, base, state, denominator):
    orb_rows, virt, _ = state.shape
    count = rows * orb_rows
    return pl.pallas_call(
        functools.partial(update_body, rows, halves),
        out_shape=(
            jax.ShapeDtypeStruct((orb_rows, virt, virt), jnp.float32),
            jax.ShapeDtypeStruct((orb_rows, virt, virt), jnp.bfloat16),
        ),
        in_specs=[SMEM] + [ANY] * (rows + 2 * halves) + [VMEM] * 3,
        out_specs=(VMEM, VMEM),
        scratch_shapes=[
            pltpu.VMEM((count, virt, virt), jnp.bfloat16),
            pltpu.VMEM((2 * halves, orb_rows, virt, virt), jnp.bfloat16),
            pltpu.VMEM((orb_rows, virt, virt), jnp.float32),
            pltpu.SemaphoreType.DMA((rows,)),
            pltpu.SemaphoreType.DMA((2 * halves,)),
        ],
        compiler_params=pltpu.CompilerParams(vmem_limit_bytes=VMEM_BYTES),
        cost_estimate=pl.CostEstimate(
            flops=2 * orb_rows * count * virt**3, bytes_accessed=2 * (orb_rows + 1) * count * virt**2, transcendentals=0
        ),
    )(meta, *c_pieces, *d_pieces, base, state, denominator)


def on_device(
    rows,
    cols,
    amplitudes,
    coulomb,
    inner_list,
    inner_count,
    reader_list,
    reader_count,
    virtual_energy,
    occupied_energy,
):
    orb_rows, orb_cols, virt, _ = amplitudes.shape
    count = coulomb.shape[1]
    slots = inner_list.shape[2]
    assert orb_cols == 1 and count == cols == rows * orb_rows and orb_rows == 2
    halves = cols // 2
    my_row = lax.axis_index("row")
    my_col = lax.axis_index("col")

    def from_row(x, step):
        return lax.ppermute(x, "row", [(r ^ step, r) for r in range(rows)])

    def from_col(x, at):
        return lax.ppermute(x, "col", [(c ^ at, c) for c in range(cols)])

    def mirrored(x, flip):
        pairs = []
        for r in range(rows):
            for c in range(cols):
                i = 2 * r + ((c % 2) ^ flip)
                pairs.append((r * cols + c, (c // 2) * cols + i))
        return lax.ppermute(x, ("row", "col"), pairs)

    state = amplitudes[:, 0]
    half = state.astype(jnp.bfloat16)

    slot_iota = jnp.arange(slots, dtype=jnp.int32)
    orbital_iota = jnp.arange(count, dtype=jnp.int32)

    def used(lists, counts):
        live = slot_iota[None] < counts[:, None]
        hit = (lists[:, :, None] == orbital_iota) & live[:, :, None]
        return jnp.any(hit, axis=1).astype(jnp.int32)

    inner_used = used(inner_list[:, 0], inner_count[:, 0])
    reader_used = used(
        lax.dynamic_index_in_dim(reader_list, my_col, 1, False), lax.dynamic_index_in_dim(reader_count, my_col, 1, False)
    )
    place = jnp.where(orbital_iota == 0, my_row, my_col).astype(jnp.int32)
    meta = jnp.concatenate([inner_used, reader_used, place[None]], axis=0)

    occ_rows = lax.dynamic_slice_in_dim(occupied_energy, my_row * orb_rows, orb_rows, 0)
    occ_col = lax.dynamic_slice_in_dim(occupied_energy, my_col, 1, 0)
    virt_pair = virtual_energy[:, None] + virtual_energy[None, :]
    denominator = virt_pair[None] - occ_rows[:, None, None] - occ_col[:, None, None]
    coulomb_own = lax.dynamic_index_in_dim(coulomb, my_col, 1, False).astype(jnp.float32)
    parity = my_col % 2

    for sweep_index in range(ITERS):
        a_pieces = [half] + [from_row(half, step) for step in range(1, rows)]
        d_own = [half] + [from_col(half, 2 * at) for at in range(1, halves)]
        d_pieces = []
        for piece in d_own:
            d_pieces += [piece, from_col(piece, 1)]
        coupled = coupled_blocks(rows, meta, coulomb, a_pieces)
        c_pieces = [coupled] + [from_row(coupled, step) for step in range(1, rows)]
        near = mirrored(lax.dynamic_index_in_dim(coupled, parity, 0, False), 0)
        far = mirrored(lax.dynamic_index_in_dim(coupled, 1 - parity, 0, False), 1)
        first = jnp.where(parity == 0, near, far)
        second = jnp.where(parity == 0, far, near)
        mirror = jnp.transpose(jnp.stack([first, second]), (0, 2, 1))
        base = coulomb_own + coupling * (coupled.astype(jnp.float32) + mirror.astype(jnp.float32))
        state, half = updated_state(rows, halves, meta, c_pieces, d_pieces, base, state, denominator)
    return state[:, None]


def solution(mesh):
    return jax.shard_map(
        functools.partial(on_device, mesh.shape["row"], mesh.shape["col"]),
        mesh=mesh,
        in_specs=(
            P("row", "col", None, None),
            P("row", None, None, None),
            P("row", "col", None),
            P("row", "col"),
            P("row", None, None),
            P("row", None),
            P(),
            P(),
        ),
        out_specs=P("row", "col", None, None),
        check_vma=False,
    )
```

time: 255 us -> 127 us (0.50)
  the two profiles are of different devices: /device:TPU:7 before, /device:TPU:0 now
where the time goes in v1:
time: 127 us
  starting transfers between devices  52.4 us (41%)
  waiting for transfers between devices  43.1 us (34%)
  Pallas kernels  18.6 us (15%)
  local copies, waits for them, and re-layouts  6.8 us (5%)
  other arithmetic  6.34 us (5%)
    ppermute x12, starting transfers between devices, from_row(): return lax.ppermute(x, 'row', [(r ^ step, r) for r in range(rows)])  28.9 us
    ppermute x14, waiting for transfers between devices, from_col(): return lax.ppermute(x, 'col', [(c ^ at, c) for c in range(cols)])  26.2 us
    ppermute x14, starting transfers between devices, from_col(): return lax.ppermute(x, 'col', [(c ^ at, c) for c in range(cols)])  22.1 us
    ppermute x12, waiting for transfers between devices, from_row(): return lax.ppermute(x, 'row', [(r ^ step, r) for r in range(rows)])  16.8 us
    pallas_call x2, Pallas kernels, updated_state(): pl.pallas_call(functools.partial(update_body, rows, halves), out_shape=(j...  11.3 us
    pallas_call x2, Pallas kernels, coupled_blocks(): pl.pallas_call(functools.partial(coupled_body, rows), out_shape=jax.Shape...  7.23 us
    unnamed x12, local copies, waits for them, and re-layouts  3.43 us
  transfers between devices with their start and end apart: 30, of which 14 were waited for; matrix products, arithmetic and copies ran while one was open for 7% of the time, Pallas kernels for 6%

profile of v1, /device:TPU:0, one launch (start us, length us, event | category | flops | bytes accessed | tf_op | source)
XLA Modules:
  0.0 127.4 jit_solution(17352641500184880281)
XLA Ops:
  0.0 1.1 bitcast_convert_fusion.refs_0_.refs_4_
  1.1 5.1 %collective-permute-start.11 = (bf16[2,256,256]{2,1,0:T(8,128)(2,1)S(1)}, bf16[2,256,256]{2,1,0:T(8,128)(2,1)}, u32[]{:S(2)}, u32[]{:S(2)}) collective-permute-start(bf16[2,256,256]{2,1,0:T(8,128)(2,1)S(1)} %bitcast_convert_fusion.refs_0_.refs_4_), channel_id=1, source_target_pairs={{6,0},{7,1},{4,2},{5,3},{2,4},{3,5},{0,6},{1,7},{14,8},{15,9},{12,... | collective-permute-start | bytes 786440 | tf_op jit(solution)/shard_map/ppermute | solution.py:153
  6.2 2.4 %collective-permute-start.2 = (bf16[2,256,256]{2,1,0:T(8,128)(2,1)S(1)}, bf16[2,256,256]{2,1,0:T(8,128)(2,1)S(1)}, u32[]{:S(2)}, u32[]{:S(2)}) collective-permute-start(bf16[2,256,256]{2,1,0:T(8,128)(2,1)S(1)} %bitcast_convert_fusion.refs_0_.refs_4_), channel_id=1, source_target_pairs={{24,0},{16,8},{8,16},{0,24},{25,1},{17,9},{9,17},{1,25},{26,2},{18... | collective-permute-start | bytes 786440 | tf_op jit(solution)/shard_map/ppermute | solution.py:150
  10.4 0.9 fusion.6
  11.4 1.6 %broadcast_add_fusion = f32[256,256]{1,0:T(8,128)} fusion(f32[256]{0:T(256)} %param.14), kind=kLoop, calls=%fused_computation.9 | loop fusion | flops 65536 | bytes 263168 | tf_op jit(solution)/shard_map/add | solution.py:183
  13.8 1.3 %dynamic_slice.40 = f32[1]{0:T(128)} dynamic-slice(f32[8]{0:T(128)} %param.15, s32[]{:T(128)S(6)} %select_n.59), dynamic_slice_sizes={1} | dynamic-slice | bytes 12 | tf_op jit(solution)/shard_map/dynamic_slice | solution.py:182
  15.9 8.6 %collective-permute-start.7 = (bf16[2,256,256]{2,1,0:T(8,128)(2,1)S(1)}, bf16[2,256,256]{2,1,0:T(8,128)(2,1)}, u32[]{:S(2)}, u32[]{:S(2)}) collective-permute-start(bf16[2,256,256]{2,1,0:T(8,128)(2,1)S(1)} %bitcast_convert_fusion.refs_0_.refs_4_), channel_id=1, source_target_pairs={{2,0},{3,1},{0,2},{1,3},{6,4},{7,5},{4,6},{5,7},{10,8},{11,9},{8,1... | collective-permute-start | bytes 786440 | tf_op jit(solution)/shard_map/ppermute | solution.py:153
  25.0 1.6 %copy-done.1 = bf16[2,8,256,256]{3,2,1,0:T(8,128)(2,1)S(1)} copy-done((bf16[2,8,256,256]{3,2,1,0:T(8,128)(2,1)S(1)}, bf16[2,8,256,256]{3,2,1,0:T(8,128)(2,1)}, u32[]{:S(2)}) %copy-start.1) | copy-done | bytes 2097176
  26.6 3.6 %shard_map.85.refs_0_ = bf16[2,256,256]{2,1,0:T(8,128)(2,1)S(1)} custom-call(s32[5,8]{1,0:T(8,128)S(1)} %pad_add_fusion.meta, bf16[2,8,256,256]{3,2,1,0:T(8,128)(2,1)S(1)} %copy-done.1, bf16[2,256,256]{2,1,0:T(8,128)(2,1)S(1)} %bitcast_convert_fusion.refs_0_.refs_4_, bf16[2,256,256]{2,1,0:T(8,128)(2,1)S(1)} %collective-permute-done.refs_1_, ...), custom_call_target="tpu_custom_call" | custom-call | flops 536870912 | bytes 3145728 | tf_op jit(solution)/shard_map/pallas_call | solution.py:51
  31.3 1.7 %subtract_subtract_fusion.refs_14_ = f32[2,256,256]{2,1,0:T(8,128)S(1)} fusion(f32[]{:T(128)} %bitcast.10, f32[2]{0:T(128)S(1)} %dynamic_slice.39, f32[256,256]{1,0:T(8,128)} %broadcast_add_fusion), kind=kLoop, calls=%fused_computation.6 | loop fusion | flops 262144 | bytes 786444 | tf_op jit(solution)/shard_map/sub | solution.py:184
  33.0 1.1 collective-permute-done.7.refs_6_
  34.1 7.4 %collective-permute-start.5 = (bf16[2,256,256]{2,1,0:T(8,128)(2,1)S(1)}, bf16[2,256,256]{2,1,0:T(8,128)(2,1)S(1)}, u32[]{:S(2)}, u32[]{:S(2)}) collective-permute-start(bf16[2,256,256]{2,1,0:T(8,128)(2,1)S(1)} %shard_map.85.refs_0_), channel_id=1, source_target_pairs={{24,0},{16,8},{8,16},{0,24},{25,1},{17,9},{9,17},{1,25},{26,2},{18... | collective-permute-start | bytes 786440 | tf_op jit(solution)/shard_map/ppermute | solution.py:150
  41.5 8.3 %collective-permute-start.3 = (bf16[2,256,256]{2,1,0:T(8,128)(2,1)S(1)}, bf16[2,256,256]{2,1,0:T(8,128)(2,1)S(1)}, u32[]{:S(2)}, u32[]{:S(2)}) collective-permute-start(bf16[2,256,256]{2,1,0:T(8,128)(2,1)S(1)} %shard_map.85.refs_0_), channel_id=1, source_target_pairs={{8,0},{0,8},{24,16},{16,24},{9,1},{1,9},{25,17},{17,25},{10,2},{2,... | collective-permute-start | bytes 786440 | tf_op jit(solution)/shard_map/ppermute | solution.py:150
  50.5 1.1 collective-permute-done.10.refs_9_
  52.0 1.8 %collective-permute-done.5.refs_3_ = bf16[2,256,256]{2,1,0:T(8,128)(2,1)S(1)} collective-permute-done((bf16[2,256,256]{2,1,0:T(8,128)(2,1)S(1)}, bf16[2,256,256]{2,1,0:T(8,128)(2,1)S(1)}, u32[]{:S(2)}, u32[]{:S(2)}) %collective-permute-start.5) | collective-permute-done | bytes 262176 | tf_op jit(solution)/shard_map/ppermute | solution.py:150
  54.2 5.1 %collective-permute-done.3.refs_1_ = bf16[2,256,256]{2,1,0:T(8,128)(2,1)S(1)} collective-permute-done((bf16[2,256,256]{2,1,0:T(8,128)(2,1)S(1)}, bf16[2,256,256]{2,1,0:T(8,128)(2,1)S(1)}, u32[]{:S(2)}, u32[]{:S(2)}) %collective-permute-start.3) | collective-permute-done | bytes 262176 | tf_op jit(solution)/shard_map/ppermute | solution.py:150
  59.3 1.0 copy-done.3
  60.3 5.2 %shard_map.86 = (f32[2,256,256]{2,1,0:T(8,128)S(1)}, bf16[2,256,256]{2,1,0:T(8,128)(2,1)S(1)}) custom-call(s32[5,8]{1,0:T(8,128)S(1)} %pad_add_fusion.meta, bf16[2,256,256]{2,1,0:T(8,128)(2,1)S(1)} %shard_map.85.refs_0_, bf16[2,256,256]{2,1,0:T(8,128)(2,1)S(1)} %collective-permute-done.3.refs_1_, bf16[2,256,256]{2,1,0:T(8,128)(2,1)S(1)} %collective-permute-done.4.refs_2_, ...), custom_call_target="tpu_custom_call" | custom-call | flops 536870912 | bytes 3145728 | tf_op jit(solution)/shard_map/pallas_call | solution.py:107
  65.6 0.8 copy-done.4
  66.4 3.3 %collective-permute-start.17 = (bf16[2,256,256]{2,1,0:T(8,128)(2,1)S(1)}, bf16[2,256,256]{2,1,0:T(8,128)(2,1)S(1)}, u32[]{:S(2)}, u32[]{:S(2)}) collective-permute-start(bf16[2,256,256]{2,1,0:T(8,128)(2,1)S(1)} %get-tuple-element.8.refs_0_.refs_4_), channel_id=1, source_target_pairs={{24,0},{16,8},{8,16},{0,24},{25,1},{17,9},{9,17},{1,25},{26,2},{18... | collective-permute-start | bytes 786440 | tf_op jit(solution)/shard_map/ppermute | solution.py:150
  69.7 0.8 collective-permute-start.16
  70.5 1.5 %collective-permute-start.15 = (bf16[2,256,256]{2,1,0:T(8,128)(2,1)S(1)}, bf16[2,256,256]{2,1,0:T(8,128)(2,1)S(1)}, u32[]{:S(2)}, u32[]{:S(2)}) collective-permute-start(bf16[2,256,256]{2,1,0:T(8,128)(2,1)S(1)} %get-tuple-element.8.refs_0_.refs_4_), channel_id=1, source_target_pairs={{8,0},{0,8},{24,16},{16,24},{9,1},{1,9},{25,17},{17,25},{10,2},{2,... | collective-permute-start | bytes 786440 | tf_op jit(solution)/shard_map/ppermute | solution.py:150
  72.0 5.6 %collective-permute-done.26.refs_10_ = bf16[2,256,256]{2,1,0:T(8,128)(2,1)} collective-permute-done((bf16[2,256,256]{2,1,0:T(8,128)(2,1)S(1)}, bf16[2,256,256]{2,1,0:T(8,128)(2,1)}, u32[]{:S(2)}, u32[]{:S(2)}) %collective-permute-start.26) | collective-permute-done | bytes 262176 | tf_op jit(solution)/shard_map/ppermute | solution.py:153
  77.6 6.3 %collective-permute-start.22 = (bf16[2,256,256]{2,1,0:T(8,128)(2,1)S(1)}, bf16[2,256,256]{2,1,0:T(8,128)(2,1)}, u32[]{:S(2)}, u32[]{:S(2)}) collective-permute-start(bf16[2,256,256]{2,1,0:T(8,128)(2,1)S(1)} %get-tuple-element.8.refs_0_.refs_4_), channel_id=1, source_target_pairs={{2,0},{3,1},{0,2},{1,3},{6,4},{7,5},{4,6},{5,7},{10,8},{11,9},{8,1... | collective-permute-start | bytes 786440 | tf_op jit(solution)/shard_map/ppermute | solution.py:153
  84.4 3.6 %shard_map.87.refs_0_ = bf16[2,256,256]{2,1,0:T(8,128)(2,1)S(1)} custom-call(s32[5,8]{1,0:T(8,128)S(1)} %pad_add_fusion.meta, bf16[2,8,256,256]{3,2,1,0:T(8,128)(2,1)S(1)} %copy-done.2, bf16[2,256,256]{2,1,0:T(8,128)(2,1)S(1)} %get-tuple-element.8.refs_0_.refs_4_, bf16[2,256,256]{2,1,0:T(8,128)(2,1)S(1)} %collective-permute-done.15.refs_1_, ...), custom_call_target="tpu_custom_call" | custom-call | flops 536870912 | bytes 3145728 | tf_op jit(solution)/shard_map/pallas_call | solution.py:51
  89.5 16.2 %collective-permute-done.22.refs_6_ = bf16[2,256,256]{2,1,0:T(8,128)(2,1)} collective-permute-done((bf16[2,256,256]{2,1,0:T(8,128)(2,1)S(1)}, bf16[2,256,256]{2,1,0:T(8,128)(2,1)}, u32[]{:S(2)}, u32[]{:S(2)}) %collective-permute-start.22) | collective-permute-done | bytes 262176 | tf_op jit(solution)/shard_map/ppermute | solution.py:153
  105.7 4.0 %collective-permute-start.18 = (bf16[2,256,256]{2,1,0:T(8,128)(2,1)S(1)}, bf16[2,256,256]{2,1,0:T(8,128)(2,1)S(1)}, u32[]{:S(2)}, u32[]{:S(2)}) collective-permute-start(bf16[2,256,256]{2,1,0:T(8,128)(2,1)S(1)} %shard_map.87.refs_0_), channel_id=1, source_target_pairs={{8,0},{0,8},{24,16},{16,24},{9,1},{1,9},{25,17},{17,25},{10,2},{2,... | collective-permute-start | bytes 786440 | tf_op jit(solution)/shard_map/ppermute | solution.py:150
  110.4 1.1 collective-permute-done.25.refs_9_
  111.9 3.9 %collective-permute-done.20.refs_3_ = bf16[2,256,256]{2,1,0:T(8,128)(2,1)S(1)} collective-permute-done((bf16[2,256,256]{2,1,0:T(8,128)(2,1)S(1)}, bf16[2,256,256]{2,1,0:T(8,128)(2,1)S(1)}, u32[]{:S(2)}, u32[]{:S(2)}) %collective-permute-start.20) | collective-permute-done | bytes 262176 | tf_op jit(solution)/shard_map/ppermute | solution.py:150
  115.8 3.6 %collective-permute-done.19.refs_2_ = bf16[2,256,256]{2,1,0:T(8,128)(2,1)S(1)} collective-permute-done((bf16[2,256,256]{2,1,0:T(8,128)(2,1)S(1)}, bf16[2,256,256]{2,1,0:T(8,128)(2,1)S(1)}, u32[]{:S(2)}, u32[]{:S(2)}) %collective-permute-start.19) | collective-permute-done | bytes 262176 | tf_op jit(solution)/shard_map/ppermute | solution.py:150
  119.4 1.9 %collective-permute-done.18.refs_1_ = bf16[2,256,256]{2,1,0:T(8,128)(2,1)S(1)} collective-permute-done((bf16[2,256,256]{2,1,0:T(8,128)(2,1)S(1)}, bf16[2,256,256]{2,1,0:T(8,128)(2,1)S(1)}, u32[]{:S(2)}, u32[]{:S(2)}) %collective-permute-start.18) | collective-permute-done | bytes 262176 | tf_op jit(solution)/shard_map/ppermute | solution.py:150
  121.3 6.1 %shard_map.88 = (f32[2,256,256]{2,1,0:T(8,128)}, bf16[2,256,256]{2,1,0:T(8,128)(2,1)}) custom-call(s32[5,8]{1,0:T(8,128)S(1)} %pad_add_fusion.meta, bf16[2,256,256]{2,1,0:T(8,128)(2,1)S(1)} %shard_map.87.refs_0_, bf16[2,256,256]{2,1,0:T(8,128)(2,1)S(1)} %collective-permute-done.18.refs_1_, bf16[2,256,256]{2,1,0:T(8,128)(2,1)S(1)} %collective-permute-done.19.refs_2_, ...), custom_call_target="tpu_custom_call" | custom-call | flops 536870912 | bytes 3145728 | tf_op jit(solution)/shard_map/pallas_call | solution.py:107
  (69 shorter events, 9.5 us)
Async XLA Ops:
  1.1 14.8 %collective-permute-start.11 = (bf16[2,256,256]{2,1,0:T(8,128)(2,1)S(1)}, bf16[2,256,256]{2,1,0:T(8,128)(2,1)}, u32[]{:S(2)}, u32[]{:S(2)}) collective-permute-start(bf16[2,256,256]{2,1,0:T(8,128)(2,1)S(1)} %bitcast_convert_fusion.refs_0_.refs_4_), channel_id=1, source_target_pairs={{6,0},{7,1},{4,2},{5,3},{2,4},{3,5},{0,6},{1,7},{14,8},{15,9},{12,... | collective-permute-start | bytes 786440 | tf_op jit(solution)/shard_map/ppermute | solution.py:153
  6.2 24.4 %collective-permute-start.9 = (bf16[2,256,256]{2,1,0:T(8,128)(2,1)S(1)}, bf16[2,256,256]{2,1,0:T(8,128)(2,1)}, u32[]{:S(2)}, u32[]{:S(2)}) collective-permute-start(bf16[2,256,256]{2,1,0:T(8,128)(2,1)S(1)} %bitcast_convert_fusion.refs_0_.refs_4_), channel_id=1, source_target_pairs={{4,0},{5,1},{6,2},{7,3},{0,4},{1,5},{2,6},{3,7},{12,8},{13,9},{14,... | collective-permute-start | bytes 786440 | tf_op jit(solution)/shard_map/ppermute | solution.py:153
  6.2 18.3 %collective-permute-start.2 = (bf16[2,256,256]{2,1,0:T(8,128)(2,1)S(1)}, bf16[2,256,256]{2,1,0:T(8,128)(2,1)S(1)}, u32[]{:S(2)}, u32[]{:S(2)}) collective-permute-start(bf16[2,256,256]{2,1,0:T(8,128)(2,1)S(1)} %bitcast_convert_fusion.refs_0_.refs_4_), channel_id=1, source_target_pairs={{24,0},{16,8},{8,16},{0,24},{25,1},{17,9},{9,17},{1,25},{26,2},{18... | collective-permute-start | bytes 786440 | tf_op jit(solution)/shard_map/ppermute | solution.py:150
  8.7 15.9 %collective-permute-start.1 = (bf16[2,256,256]{2,1,0:T(8,128)(2,1)S(1)}, bf16[2,256,256]{2,1,0:T(8,128)(2,1)S(1)}, u32[]{:S(2)}, u32[]{:S(2)}) collective-permute-start(bf16[2,256,256]{2,1,0:T(8,128)(2,1)S(1)} %bitcast_convert_fusion.refs_0_.refs_4_), channel_id=1, source_target_pairs={{16,0},{24,8},{0,16},{8,24},{17,1},{25,9},{1,17},{9,25},{18,2},{26... | collective-permute-start | bytes 786440 | tf_op jit(solution)/shard_map/ppermute | solution.py:150
  9.2 15.9 %collective-permute-start = (bf16[2,256,256]{2,1,0:T(8,128)(2,1)S(1)}, bf16[2,256,256]{2,1,0:T(8,128)(2,1)S(1)}, u32[]{:S(2)}, u32[]{:S(2)}) collective-permute-start(bf16[2,256,256]{2,1,0:T(8,128)(2,1)S(1)} %bitcast_convert_fusion.refs_0_.refs_4_), channel_id=1, source_target_pairs={{8,0},{0,8},{24,16},{16,24},{9,1},{1,9},{25,17},{17,25},{10,2},{2,... | collective-permute-start | bytes 786440 | tf_op jit(solution)/shard_map/ppermute | solution.py:150
  15.9 18.2 %collective-permute-start.7 = (bf16[2,256,256]{2,1,0:T(8,128)(2,1)S(1)}, bf16[2,256,256]{2,1,0:T(8,128)(2,1)}, u32[]{:S(2)}, u32[]{:S(2)}) collective-permute-start(bf16[2,256,256]{2,1,0:T(8,128)(2,1)S(1)} %bitcast_convert_fusion.refs_0_.refs_4_), channel_id=1, source_target_pairs={{2,0},{3,1},{0,2},{1,3},{6,4},{7,5},{4,6},{5,7},{10,8},{11,9},{8,1... | collective-permute-start | bytes 786440 | tf_op jit(solution)/shard_map/ppermute | solution.py:153
  24.5 17.0 %collective-permute-start.6 = (bf16[2,256,256]{2,1,0:T(8,128)(2,1)S(1)}, bf16[2,256,256]{2,1,0:T(8,128)(2,1)}, u32[]{:S(2)}, u32[]{:S(2)}) collective-permute-start(bf16[2,256,256]{2,1,0:T(8,128)(2,1)S(1)} %bitcast_convert_fusion.refs_0_.refs_4_), channel_id=1, source_target_pairs={{1,0},{0,1},{3,2},{2,3},{5,4},{4,5},{7,6},{6,7},{9,8},{8,9},{11,10... | collective-permute-start | bytes 786440 | tf_op jit(solution)/shard_map/ppermute | solution.py:153
  24.5 25.3 %collective-permute-start.12 = (bf16[2,256,256]{2,1,0:T(8,128)(2,1)}, bf16[2,256,256]{2,1,0:T(8,128)(2,1)}, u32[]{:S(2)}, u32[]{:S(2)}) collective-permute-start(bf16[2,256,256]{2,1,0:T(8,128)(2,1)} %collective-permute-done.11.refs_10_), channel_id=1, source_target_pairs={{1,0},{0,1},{3,2},{2,3},{5,4},{4,5},{7,6},{6,7},{9,8},{8,9},{11,10... | collective-permute-start | bytes 786440 | tf_op jit(solution)/shard_map/ppermute | solution.py:153
  26.6 23.7 %copy-start.2 = (bf16[2,8,256,256]{3,2,1,0:T(8,128)(2,1)S(1)}, bf16[2,8,256,256]{3,2,1,0:T(8,128)(2,1)}, u32[]{:S(2)}) copy-start(bf16[2,8,256,256]{3,2,1,0:T(8,128)(2,1)} %k_hbm.3) | copy-start | bytes 6291460
  30.5 11.0 %collective-permute-start.14 = (bf16[256,256]{0,1:T(8,128)(2,1)S(1)}, bf16[256,256]{0,1:T(8,128)(2,1)S(1)}, u32[]{:S(2)}, u32[]{:S(2)}) collective-permute-start(bf16[256,256]{0,1:T(8,128)(2,1)S(1)} %bitcast.42), channel_id=1, source_target_pairs={{0,1},{1,0},{2,9},{3,8},{4,17},{5,16},{6,25},{7,24},{8,3},{9,2},{1... | collective-permute-start | bytes 393224 | tf_op jit(solution)/shard_map/ppermute | solution.py:161
  30.6 19.2 %collective-permute-start.13 = (bf16[256,256]{0,1:T(8,128)(2,1)S(1)}, bf16[256,256]{0,1:T(8,128)(2,1)S(1)}, u32[]{:S(2)}, u32[]{:S(2)}) collective-permute-start(bf16[256,256]{0,1:T(8,128)(2,1)S(1)} %bitcast.40), channel_id=1, source_target_pairs={{0,0},{1,1},{2,8},{3,9},{4,16},{5,17},{6,24},{7,25},{8,2},{9,3},{1... | collective-permute-start | bytes 393224 | tf_op jit(solution)/shard_map/ppermute | solution.py:161
  34.1 19.6 %collective-permute-start.5 = (bf16[2,256,256]{2,1,0:T(8,128)(2,1)S(1)}, bf16[2,256,256]{2,1,0:T(8,128)(2,1)S(1)}, u32[]{:S(2)}, u32[]{:S(2)}) collective-permute-start(bf16[2,256,256]{2,1,0:T(8,128)(2,1)S(1)} %shard_map.85.refs_0_), channel_id=1, source_target_pairs={{24,0},{16,8},{8,16},{0,24},{25,1},{17,9},{9,17},{1,25},{26,2},{18... | collective-permute-start | bytes 786440 | tf_op jit(solution)/shard_map/ppermute | solution.py:150
  41.5 12.7 %collective-permute-start.4 = (bf16[2,256,256]{2,1,0:T(8,128)(2,1)S(1)}, bf16[2,256,256]{2,1,0:T(8,128)(2,1)S(1)}, u32[]{:S(2)}, u32[]{:S(2)}) collective-permute-start(bf16[2,256,256]{2,1,0:T(8,128)(2,1)S(1)} %shard_map.85.refs_0_), channel_id=1, source_target_pairs={{16,0},{24,8},{0,16},{8,24},{17,1},{25,9},{1,17},{9,25},{18,2},{26... | collective-permute-start | bytes 786440 | tf_op jit(solution)/shard_map/ppermute | solution.py:150
  41.5 17.8 %collective-permute-start.3 = (bf16[2,256,256]{2,1,0:T(8,128)(2,1)S(1)}, bf16[2,256,256]{2,1,0:T(8,128)(2,1)S(1)}, u32[]{:S(2)}, u32[]{:S(2)}) collective-permute-start(bf16[2,256,256]{2,1,0:T(8,128)(2,1)S(1)} %shard_map.85.refs_0_), channel_id=1, source_target_pairs={{8,0},{0,8},{24,16},{16,24},{9,1},{1,9},{25,17},{17,25},{10,2},{2,... | collective-permute-start | bytes 786440 | tf_op jit(solution)/shard_map/ppermute | solution.py:150
  49.8 1.7 %collective-permute-start.10 = (bf16[2,256,256]{2,1,0:T(8,128)(2,1)}, bf16[2,256,256]{2,1,0:T(8,128)(2,1)S(1)}, u32[]{:S(2)}, u32[]{:S(2)}) collective-permute-start(bf16[2,256,256]{2,1,0:T(8,128)(2,1)} %collective-permute-done.9.refs_8_), channel_id=1, source_target_pairs={{1,0},{0,1},{3,2},{2,3},{5,4},{4,5},{7,6},{6,7},{9,8},{8,9},{11,10... | collective-permute-start | bytes 786440 | tf_op jit(solution)/shard_map/ppermute | solution.py:153
  49.8 2.1 %collective-permute-start.8 = (bf16[2,256,256]{2,1,0:T(8,128)(2,1)}, bf16[2,256,256]{2,1,0:T(8,128)(2,1)S(1)}, u32[]{:S(2)}, u32[]{:S(2)}) collective-permute-start(bf16[2,256,256]{2,1,0:T(8,128)(2,1)} %collective-permute-done.7.refs_6_), channel_id=1, source_target_pairs={{1,0},{0,1},{3,2},{2,3},{5,4},{4,5},{7,6},{6,7},{9,8},{8,9},{11,10... | collective-permute-start | bytes 786440 | tf_op jit(solution)/shard_map/ppermute | solution.py:153
  66.4 11.2 %collective-permute-start.26 = (bf16[2,256,256]{2,1,0:T(8,128)(2,1)S(1)}, bf16[2,256,256]{2,1,0:T(8,128)(2,1)}, u32[]{:S(2)}, u32[]{:S(2)}) collective-permute-start(bf16[2,256,256]{2,1,0:T(8,128)(2,1)S(1)} %get-tuple-element.8.refs_0_.refs_4_), channel_id=1, source_target_pairs={{6,0},{7,1},{4,2},{5,3},{2,4},{3,5},{0,6},{1,7},{14,8},{15,9},{12,... | collective-permute-start | bytes 786440 | tf_op jit(solution)/shard_map/ppermute | solution.py:153
  66.4 17.5 %collective-permute-start.17 = (bf16[2,256,256]{2,1,0:T(8,128)(2,1)S(1)}, bf16[2,256,256]{2,1,0:T(8,128)(2,1)S(1)}, u32[]{:S(2)}, u32[]{:S(2)}) collective-permute-start(bf16[2,256,256]{2,1,0:T(8,128)(2,1)S(1)} %get-tuple-element.8.refs_0_.refs_4_), channel_id=1, source_target_pairs={{24,0},{16,8},{8,16},{0,24},{25,1},{17,9},{9,17},{1,25},{26,2},{18... | collective-permute-start | bytes 786440 | tf_op jit(solution)/shard_map/ppermute | solution.py:150
  69.7 14.2 %collective-permute-start.16 = (bf16[2,256,256]{2,1,0:T(8,128)(2,1)S(1)}, bf16[2,256,256]{2,1,0:T(8,128)(2,1)S(1)}, u32[]{:S(2)}, u32[]{:S(2)}) collective-permute-start(bf16[2,256,256]{2,1,0:T(8,128)(2,1)S(1)} %get-tuple-element.8.refs_0_.refs_4_), channel_id=1, source_target_pairs={{16,0},{24,8},{0,16},{8,24},{17,1},{25,9},{1,17},{9,25},{18,2},{26... | collective-permute-start | bytes 786440 | tf_op jit(solution)/shard_map/ppermute | solution.py:150
  70.5 13.9 %collective-permute-start.15 = (bf16[2,256,256]{2,1,0:T(8,128)(2,1)S(1)}, bf16[2,256,256]{2,1,0:T(8,128)(2,1)S(1)}, u32[]{:S(2)}, u32[]{:S(2)}) collective-permute-start(bf16[2,256,256]{2,1,0:T(8,128)(2,1)S(1)} %get-tuple-element.8.refs_0_.refs_4_), channel_id=1, source_target_pairs={{8,0},{0,8},{24,16},{16,24},{9,1},{1,9},{25,17},{17,25},{10,2},{2,... | collective-permute-start | bytes 786440 | tf_op jit(solution)/shard_map/ppermute | solution.py:150
  72.0 16.9 %collective-permute-start.24 = (bf16[2,256,256]{2,1,0:T(8,128)(2,1)S(1)}, bf16[2,256,256]{2,1,0:T(8,128)(2,1)}, u32[]{:S(2)}, u32[]{:S(2)}) collective-permute-start(bf16[2,256,256]{2,1,0:T(8,128)(2,1)S(1)} %get-tuple-element.8.refs_0_.refs_4_), channel_id=1, source_target_pairs={{4,0},{5,1},{6,2},{7,3},{0,4},{1,5},{2,6},{3,7},{12,8},{13,9},{14,... | collective-permute-start | bytes 786440 | tf_op jit(solution)/shard_map/ppermute | solution.py:153
  77.6 28.1 %collective-permute-start.22 = (bf16[2,256,256]{2,1,0:T(8,128)(2,1)S(1)}, bf16[2,256,256]{2,1,0:T(8,128)(2,1)}, u32[]{:S(2)}, u32[]{:S(2)}) collective-permute-start(bf16[2,256,256]{2,1,0:T(8,128)(2,1)S(1)} %get-tuple-element.8.refs_0_.refs_4_), channel_id=1, source_target_pairs={{2,0},{3,1},{0,2},{1,3},{6,4},{7,5},{4,6},{5,7},{10,8},{11,9},{8,1... | collective-permute-start | bytes 786440 | tf_op jit(solution)/shard_map/ppermute | solution.py:153
  83.9 21.8 %collective-permute-start.21 = (bf16[2,256,256]{2,1,0:T(8,128)(2,1)S(1)}, bf16[2,256,256]{2,1,0:T(8,128)(2,1)}, u32[]{:S(2)}, u32[]{:S(2)}) collective-permute-start(bf16[2,256,256]{2,1,0:T(8,128)(2,1)S(1)} %get-tuple-element.8.refs_0_.refs_4_), channel_id=1, source_target_pairs={{1,0},{0,1},{3,2},{2,3},{5,4},{4,5},{7,6},{6,7},{9,8},{8,9},{11,10... | collective-permute-start | bytes 786440 | tf_op jit(solution)/shard_map/ppermute | solution.py:153
  83.9 25.9 %collective-permute-start.27 = (bf16[2,256,256]{2,1,0:T(8,128)(2,1)}, bf16[2,256,256]{2,1,0:T(8,128)(2,1)}, u32[]{:S(2)}, u32[]{:S(2)}) collective-permute-start(bf16[2,256,256]{2,1,0:T(8,128)(2,1)} %collective-permute-done.26.refs_10_), channel_id=1, source_target_pairs={{1,0},{0,1},{3,2},{2,3},{5,4},{4,5},{7,6},{6,7},{9,8},{8,9},{11,10... | collective-permute-start | bytes 786440 | tf_op jit(solution)/shard_map/ppermute | solution.py:153
  88.3 33.1 %copy-start.5 = (f32[2,256,256]{2,1,0:T(8,128)S(1)}, f32[2,256,256]{2,1,0:T(8,128)}, u32[]{:S(2)}) copy-start(f32[2,256,256]{2,1,0:T(8,128)} %copy-done.4) | copy-start | bytes 1572868
  88.3 17.4 %collective-permute-start.29 = (bf16[256,256]{0,1:T(8,128)(2,1)S(1)}, bf16[256,256]{0,1:T(8,128)(2,1)S(1)}, u32[]{:S(2)}, u32[]{:S(2)}) collective-permute-start(bf16[256,256]{0,1:T(8,128)(2,1)S(1)} %bitcast.43), channel_id=1, source_target_pairs={{0,1},{1,0},{2,9},{3,8},{4,17},{5,16},{6,25},{7,24},{8,3},{9,2},{1... | collective-permute-start | bytes 393224 | tf_op jit(solution)/shard_map/ppermute | solution.py:161
  88.8 20.9 %collective-permute-start.28 = (bf16[256,256]{0,1:T(8,128)(2,1)S(1)}, bf16[256,256]{0,1:T(8,128)(2,1)S(1)}, u32[]{:S(2)}, u32[]{:S(2)}) collective-permute-start(bf16[256,256]{0,1:T(8,128)(2,1)S(1)} %bitcast.41), channel_id=1, source_target_pairs={{0,0},{1,1},{2,8},{3,9},{4,16},{5,17},{6,24},{7,25},{8,2},{9,3},{1... | collective-permute-start | bytes 393224 | tf_op jit(solution)/shard_map/ppermute | solution.py:161
  105.7 10.1 %collective-permute-start.20 = (bf16[2,256,256]{2,1,0:T(8,128)(2,1)S(1)}, bf16[2,256,256]{2,1,0:T(8,128)(2,1)S(1)}, u32[]{:S(2)}, u32[]{:S(2)}) collective-permute-start(bf16[2,256,256]{2,1,0:T(8,128)(2,1)S(1)} %shard_map.87.refs_0_), channel_id=1, source_target_pairs={{24,0},{16,8},{8,16},{0,24},{25,1},{17,9},{9,17},{1,25},{26,2},{18... | collective-permute-start | bytes 786440 | tf_op jit(solution)/shard_map/ppermute | solution.py:150
  105.7 13.8 %collective-permute-start.19 = (bf16[2,256,256]{2,1,0:T(8,128)(2,1)S(1)}, bf16[2,256,256]{2,1,0:T(8,128)(2,1)S(1)}, u32[]{:S(2)}, u32[]{:S(2)}) collective-permute-start(bf16[2,256,256]{2,1,0:T(8,128)(2,1)S(1)} %shard_map.87.refs_0_), channel_id=1, source_target_pairs={{16,0},{24,8},{0,16},{8,24},{17,1},{25,9},{1,17},{9,25},{18,2},{26... | collective-permute-start | bytes 786440 | tf_op jit(solution)/shard_map/ppermute | solution.py:150
  105.7 15.7 %collective-permute-start.18 = (bf16[2,256,256]{2,1,0:T(8,128)(2,1)S(1)}, bf16[2,256,256]{2,1,0:T(8,128)(2,1)S(1)}, u32[]{:S(2)}, u32[]{:S(2)}) collective-permute-start(bf16[2,256,256]{2,1,0:T(8,128)(2,1)S(1)} %shard_map.87.refs_0_), channel_id=1, source_target_pairs={{8,0},{0,8},{24,16},{16,24},{9,1},{1,9},{25,17},{17,25},{10,2},{2,... | collective-permute-start | bytes 786440 | tf_op jit(solution)/shard_map/ppermute | solution.py:150
  109.7 1.7 %collective-permute-start.25 = (bf16[2,256,256]{2,1,0:T(8,128)(2,1)}, bf16[2,256,256]{2,1,0:T(8,128)(2,1)S(1)}, u32[]{:S(2)}, u32[]{:S(2)}) collective-permute-start(bf16[2,256,256]{2,1,0:T(8,128)(2,1)} %collective-permute-done.24.refs_8_), channel_id=1, source_target_pairs={{1,0},{0,1},{3,2},{2,3},{5,4},{4,5},{7,6},{6,7},{9,8},{8,9},{11,10... | collective-permute-start | bytes 786440 | tf_op jit(solution)/shard_map/ppermute | solution.py:153
  109.7 2.1 %collective-permute-start.23 = (bf16[2,256,256]{2,1,0:T(8,128)(2,1)}, bf16[2,256,256]{2,1,0:T(8,128)(2,1)S(1)}, u32[]{:S(2)}, u32[]{:S(2)}) collective-permute-start(bf16[2,256,256]{2,1,0:T(8,128)(2,1)} %collective-permute-done.22.refs_6_), channel_id=1, source_target_pairs={{1,0},{0,1},{3,2},{2,3},{5,4},{4,5},{7,6},{6,7},{9,8},{8,9},{11,10... | collective-permute-start | bytes 786440 | tf_op jit(solution)/shard_map/ppermute | solution.py:153
  (4 other events, 14.8 us)

commit v2 on v0

v2 whole, which is shorter than its diff:
```python
import functools

import jax
import jax.numpy as jnp
from jax import lax
from jax.experimental import pallas as pl
from jax.experimental.pallas import tpu as pltpu
from jax.sharding import PartitionSpec as P

ITERS = 2


damping = 0.5
coupling = 0.03125
ANY = pl.BlockSpec(memory_space=pl.ANY)
SMEM = pl.BlockSpec(memory_space=pltpu.SMEM)
VMEM = pl.BlockSpec(memory_space=pltpu.VMEM)
VMEM_BYTES = 32 * 1024 * 1024


def call(body, out_shape, in_specs, flops, moved, *operands):
    single = isinstance(out_shape, jax.ShapeDtypeStruct)
    return pl.pallas_call(
        body,
        out_shape=out_shape,
        in_specs=in_specs,
        out_specs=VMEM if single else (VMEM,) * len(out_shape),
        compiler_params=pltpu.CompilerParams(vmem_limit_bytes=VMEM_BYTES),
        cost_estimate=pl.CostEstimate(flops=flops, bytes_accessed=moved, transcendentals=0),
    )(*operands)


def masked_coulomb_body(meta, k_ref, out_ref):
    orb_rows, _, virt, _ = k_ref.shape
    my_row = meta[2 * orb_rows, 0]
    for step in range(out_ref.shape[0]):
        for t in range(orb_rows):
            orbital = (my_row ^ step) * orb_rows + t
            for i in range(orb_rows):
                block = k_ref[i, orbital]
                keep = jnp.where(meta[i, orbital] > 0, block, jnp.zeros_like(block))
                out_ref[step, i * virt : (i + 1) * virt, t * virt : (t + 1) * virt] = keep


def masked_coulomb(rows, meta, coulomb):
    orb_rows, count, virt, _ = coulomb.shape
    shape = jax.ShapeDtypeStruct((rows, orb_rows * virt, orb_rows * virt), jnp.bfloat16)
    return call(masked_coulomb_body, shape, [SMEM, VMEM], 0, 4 * orb_rows * count * virt**2, meta, coulomb)


def coupled_body(rows, k_ref, *refs):
    out_ref = refs[rows]
    orb_rows, virt, _ = out_ref.shape
    total = None
    for step in range(rows):
        part = jnp.dot(
            k_ref[step], refs[step][...].reshape(orb_rows * virt, virt), preferred_element_type=jnp.float32
        )
        total = part if total is None else total + part
    out_ref[...] = total.astype(out_ref.dtype).reshape(out_ref.shape)


def coupled_blocks(rows, kept, pieces):
    orb_rows, virt, _ = pieces[0].shape
    count = rows * orb_rows
    shape = jax.ShapeDtypeStruct((orb_rows, virt, virt), jnp.bfloat16)
    body = functools.partial(coupled_body, rows)
    flops, moved = 2 * orb_rows * count * virt**3, 2 * (orb_rows + 1) * count * virt**2
    return call(body, shape, [VMEM] * (1 + rows), flops, moved, kept, *pieces)


def collected_body(places, meta, crossed_ref, *refs):
    out_ref = refs[len(places)]
    orb_rows = crossed_ref.shape[0]
    halves = (out_ref.shape[0] - 1) // orb_rows
    my_col = meta[2 * orb_rows, 1]
    at = my_col // 2
    for ref, hops in zip(refs, places):
        for hop in hops:
            spot = at + hop

            @pl.when(jnp.logical_and(spot >= 0, spot < halves))
            def _():
                out_ref[pl.ds(spot * orb_rows, orb_rows)] = ref[...]

    out_ref[orb_rows * halves] = crossed_ref[1 - my_col % 2]


def collected(meta, halves, crossed, pieces, places):
    orb_rows, virt, _ = crossed.shape
    shape = jax.ShapeDtypeStruct((orb_rows * halves + 1, virt, virt), jnp.bfloat16)
    body = functools.partial(collected_body, places)
    moved = 4 * (orb_rows * halves + 1) * virt**2
    return call(body, shape, [SMEM] + [VMEM] * (1 + len(pieces)), 0, moved, meta, crossed, *pieces)


def tied_body(*refs):
    pass


def tied(x, *others):
    return pl.pallas_call(
        tied_body,
        out_shape=jax.ShapeDtypeStruct(x.shape, x.dtype),
        in_specs=[ANY] * (1 + len(others)),
        out_specs=ANY,
        input_output_aliases={0: 0},
    )(x, *others)


def quadratic_part(rows, meta, side, left_ref, c_refs):
    orb_rows = c_refs[0].shape[0]
    my_row = meta[2 * orb_rows, 0]
    total = None
    for step in range(rows):
        at = my_row ^ step
        blocks = []
        for i in range(orb_rows):
            block = left_ref[at * orb_rows + i]
            blocks.append(jnp.where(meta[orb_rows + i, 2 * at + side] > 0, block, jnp.zeros_like(block)))
        part = jnp.dot(jnp.concatenate(blocks, axis=0), c_refs[step][side], preferred_element_type=jnp.float32)
        total = part if total is None else total + part
    return total.reshape(orb_rows, -1, total.shape[1])


def turned(block):
    return jnp.transpose(block.astype(jnp.float32), (1, 0))


def first_body(rows, meta, left_ref, *refs):
    c_refs = refs[:rows]
    crossed_ref, state_ref, coulomb_ref, inverse_ref, out_ref = refs[rows:]
    orb_rows = out_ref.shape[0]
    side = meta[2 * orb_rows, 1] % 2
    quadratic = quadratic_part(rows, meta, side, left_ref, c_refs)
    linear = coulomb_ref[...].astype(jnp.float32) + coupling * c_refs[0][...].astype(jnp.float32)
    residual = linear + coupling * coupling * quadratic
    out_ref[...] = damping * state_ref[...] - residual * inverse_ref[...]
    out_ref[side] -= coupling * turned(crossed_ref[side]) * inverse_ref[side]


def second_body(rows, meta, left_ref, *refs):
    c_refs = refs[:rows]
    part_ref, inverse_ref, out_ref, half_ref = refs[rows:]
    orb_rows = out_ref.shape[0]
    side = 1 - meta[2 * orb_rows, 1] % 2
    quadratic = quadratic_part(rows, meta, side, left_ref, c_refs)
    out_ref[...] = part_ref[...] - coupling * coupling * quadratic * inverse_ref[...]
    out_ref[side] -= coupling * turned(left_ref[left_ref.shape[0] - 1]) * inverse_ref[side]
    half_ref[...] = out_ref[...].astype(half_ref.dtype)


def updated_state(rows, meta, own, swapped, c_pieces, crossed, state, coulomb_own, inverse):
    orb_rows, virt, _ = state.shape
    count = rows * orb_rows
    whole = jax.ShapeDtypeStruct((orb_rows, virt, virt), jnp.float32)
    half = jax.ShapeDtypeStruct((orb_rows, virt, virt), jnp.bfloat16)
    flops, moved = orb_rows * count * virt**3, 2 * (orb_rows + 1) * count * virt**2
    part = call(
        functools.partial(first_body, rows), whole, [SMEM] + [VMEM] * (rows + 5), flops, moved,
        meta, own, *c_pieces, crossed, state, coulomb_own, inverse,
    )
    return call(
        functools.partial(second_body, rows), (whole, half), [SMEM] + [VMEM] * (rows + 3), flops, moved,
        meta, swapped, *c_pieces, part, inverse,
    )


def on_device(
    rows,
    cols,
    amplitudes,
    coulomb,
    inner_list,
    inner_count,
    reader_list,
    reader_count,
    virtual_energy,
    occupied_energy,
):
    orb_rows, orb_cols, virt, _ = amplitudes.shape
    count = coulomb.shape[1]
    slots = inner_list.shape[2]
    assert orb_cols == 1 and count == cols == rows * orb_rows and orb_rows == 2
    halves = cols // 2
    my_row = lax.axis_index("row")
    my_col = lax.axis_index("col")

    def from_row(x, step):
        return lax.ppermute(x, "row", [(r ^ step, r) for r in range(rows)])

    def along(x, hops):
        return lax.ppermute(
            x, "col", [(2 * at + k, 2 * (at + hop) + k) for at, hop in hops for k in range(2)]
        )

    def relayed(x):
        pieces, places = [x], [(0,)]
        up = down = x
        for stage in range(1, halves):
            ups = [(at, 1) for at in range(stage - 1, halves - 1)]
            downs = [(at, -1) for at in range(1, halves - stage + 1)]
            if stage - 1 > halves - stage:
                up = down = along(jnp.where(my_col // 2 >= stage - 1, up, down), ups + downs)
                pieces.append(up)
                places.append((-stage, stage))
            else:
                up, down = along(up, ups), along(down, downs)
                pieces += [up, down]
                places += [(-stage,), (stage,)]
        return pieces, tuple(places)

    def across(x):
        pairs = [(r * cols + c, (c // 2) * cols + 2 * r + c % 2) for r in range(rows) for c in range(cols)]
        return lax.ppermute(x, ("row", "col"), pairs)

    state = amplitudes[:, 0]
    half = state.astype(jnp.bfloat16)

    slot_iota = jnp.arange(slots, dtype=jnp.int32)
    orbital_iota = jnp.arange(count, dtype=jnp.int32)

    def used(lists, counts):
        live = slot_iota[None] < counts[:, None]
        hit = (lists[:, :, None] == orbital_iota) & live[:, :, None]
        return jnp.any(hit, axis=1).astype(jnp.int32)

    inner_used = used(inner_list[:, 0], inner_count[:, 0])
    reader_used = used(
        lax.dynamic_index_in_dim(reader_list, my_col, 1, False), lax.dynamic_index_in_dim(reader_count, my_col, 1, False)
    )
    place = jnp.where(orbital_iota == 0, my_row, my_col).astype(jnp.int32)
    meta = jnp.concatenate([inner_used, reader_used, place[None]], axis=0)

    occ_rows = lax.dynamic_slice_in_dim(occupied_energy, my_row * orb_rows, orb_rows, 0)
    occ_col = lax.dynamic_slice_in_dim(occupied_energy, my_col, 1, 0)
    virt_pair = virtual_energy[:, None] + virtual_energy[None, :]
    inverse = 1.0 / (virt_pair[None] - occ_rows[:, None, None] - occ_col[:, None, None])
    coulomb_own = lax.dynamic_index_in_dim(coulomb, my_col, 1, False)
    kept = masked_coulomb(rows, meta, coulomb)

    for sweep_index in range(ITERS):
        a_pieces = [half] + [from_row(half, step) for step in range(1, rows)]
        column, places = relayed(half)
        coupled = coupled_blocks(rows, kept, a_pieces)
        c_pieces = [coupled] + [from_row(coupled, step) for step in range(1, rows)]
        crossed = across(coupled)
        own = collected(meta, halves, crossed, column, places)
        own = tied(own, *c_pieces)
        swapped = lax.ppermute(own, "col", [(c ^ 1, c) for c in range(cols)])
        state, half = updated_state(rows, meta, own, swapped, c_pieces, crossed, state, coulomb_own, inverse)
    return state[:, None]


def solution(mesh):
    return jax.shard_map(
        functools.partial(on_device, mesh.shape["row"], mesh.shape["col"]),
        mesh=mesh,
        in_specs=(
            P("row", "col", None, None),
            P("row", None, None, None),
            P("row", "col", None),
            P("row", "col"),
            P("row", None, None),
            P("row", None),
            P(),
            P(),
        ),
        out_specs=P("row", "col", None, None),
        check_vma=False,
    )
```

time: 255 us -> 123 us (0.48)
  the two profiles are of different devices: /device:TPU:7 before, /device:TPU:1 now
where the time goes in v2:
time: 123 us; the launch traced here: 122 us
  waiting for transfers between devices  49.4 us (40%)
  starting transfers between devices  37.5 us (30%)
  local copies, waits for them, and re-layouts  19.9 us (16%)
  Pallas kernels  11.1 us (9%)
  other arithmetic  3.63 us (3%)
    ppermute x10, waiting for transfers between devices, along(): lax.ppermute(x, 'col', [(2 * at + k, 2 * (at + hop) + k) for at, hop in h...  43.2 us
    ppermute x12, starting transfers between devices, from_row(): return lax.ppermute(x, 'row', [(r ^ step, r) for r in range(rows)])  18.8 us
    unnamed x76, local copies, waits for them, and re-layouts  17.4 us
    ppermute x10, starting transfers between devices, along(): lax.ppermute(x, 'col', [(2 * at + k, 2 * (at + hop) + k) for at, hop in h...  14.4 us
    pallas_call x9, Pallas kernels, call(): pl.pallas_call(body, out_shape=out_shape, in_specs=in_specs, out_specs=VM...  11.1 us
    ppermute x12, waiting for transfers between devices, from_row(): return lax.ppermute(x, 'row', [(r ^ step, r) for r in range(rows)])  6.12 us
    ppermute x2, starting transfers between devices, on_device(): swapped = lax.ppermute(own, 'col', [(c ^ 1, c) for c in range(cols)])  2.91 us
  transfers between devices with their start and end apart: 26, of which 9 were waited for; matrix products, arithmetic and copies ran while one was open for 4% of the time, Pallas kernels for 6%

profile of v2, /device:TPU:1, one launch (start us, length us, event | category | flops | bytes accessed | tf_op | source)
XLA Modules:
  0.0 122.1 jit_solution(15715314437488231721)
XLA Ops:
  0.0 1.1 bitcast_convert_fusion.refs_0_
  1.1 4.0 %collective-permute-start.4 = (bf16[2,256,256]{2,1,0:T(8,128)(2,1)S(1)}, bf16[2,256,256]{2,1,0:T(8,128)(2,1)S(1)}, u32[]{:S(2)}, u32[]{:S(2)}) collective-permute-start(bf16[2,256,256]{2,1,0:T(8,128)(2,1)S(1)} %bitcast_convert_fusion.refs_0_), channel_id=1, source_target_pairs={{0,2},{1,3},{2,4},{3,5},{4,6},{5,7},{8,10},{9,11},{10,12},{11,13},... | collective-permute-start | bytes 786440 | tf_op jit(solution)/shard_map/ppermute | solution.py:193
  5.1 1.3 %collective-permute-start.5 = (bf16[2,256,256]{2,1,0:T(8,128)(2,1)S(1)}, bf16[2,256,256]{2,1,0:T(8,128)(2,1)S(1)}, u32[]{:S(2)}, u32[]{:S(2)}) collective-permute-start(bf16[2,256,256]{2,1,0:T(8,128)(2,1)S(1)} %bitcast_convert_fusion.refs_0_), channel_id=1, source_target_pairs={{2,0},{3,1},{4,2},{5,3},{6,4},{7,5},{10,8},{11,9},{12,10},{13,11},... | collective-permute-start | bytes 786440 | tf_op jit(solution)/shard_map/ppermute | solution.py:193
  6.4 1.3 %collective-permute-start = (bf16[2,256,256]{2,1,0:T(8,128)(2,1)S(1)}, bf16[2,256,256]{2,1,0:T(8,128)(2,1)S(1)}, u32[]{:S(2)}, u32[]{:S(2)}) collective-permute-start(bf16[2,256,256]{2,1,0:T(8,128)(2,1)S(1)} %bitcast_convert_fusion.refs_0_), channel_id=1, source_target_pairs={{8,0},{0,8},{24,16},{16,24},{9,1},{1,9},{25,17},{17,25},{10,2},{2,... | collective-permute-start | bytes 786440 | tf_op jit(solution)/shard_map/ppermute | solution.py:190
  7.7 1.2 %collective-permute-start.1 = (bf16[2,256,256]{2,1,0:T(8,128)(2,1)S(1)}, bf16[2,256,256]{2,1,0:T(8,128)(2,1)}, u32[]{:S(2)}, u32[]{:S(2)}) collective-permute-start(bf16[2,256,256]{2,1,0:T(8,128)(2,1)S(1)} %bitcast_convert_fusion.refs_0_), channel_id=1, source_target_pairs={{16,0},{24,8},{0,16},{8,24},{17,1},{25,9},{1,17},{9,25},{18,2},{26... | collective-permute-start | bytes 786440 | tf_op jit(solution)/shard_map/ppermute | solution.py:190
  12.4 1.6 %collective-permute-done.5.refs_2_ = bf16[2,256,256]{2,1,0:T(8,128)(2,1)S(1)} collective-permute-done((bf16[2,256,256]{2,1,0:T(8,128)(2,1)S(1)}, bf16[2,256,256]{2,1,0:T(8,128)(2,1)S(1)}, u32[]{:S(2)}, u32[]{:S(2)}) %collective-permute-start.5) | collective-permute-done | bytes 262176 | tf_op jit(solution)/shard_map/ppermute | solution.py:193
  14.0 1.3 %collective-permute-start.7 = (bf16[2,256,256]{2,1,0:T(8,128)(2,1)S(1)}, bf16[2,256,256]{2,1,0:T(8,128)(2,1)S(1)}, u32[]{:S(2)}, u32[]{:S(2)}) collective-permute-start(bf16[2,256,256]{2,1,0:T(8,128)(2,1)S(1)} %collective-permute-done.5.refs_2_), channel_id=1, source_target_pairs={{2,0},{3,1},{4,2},{5,3},{10,8},{11,9},{12,10},{13,11},{18,16},{19,... | collective-permute-start | bytes 786440 | tf_op jit(solution)/shard_map/ppermute | solution.py:193
  15.3 1.6 %copy-done.9 = bf16[2,8,256,256]{3,2,1,0:T(8,128)(2,1)S(1)} copy-done((bf16[2,8,256,256]{3,2,1,0:T(8,128)(2,1)S(1)}, bf16[2,8,256,256]{3,2,1,0:T(8,128)(2,1)}, u32[]{:S(2)}) %copy-start.9) | copy-done | bytes 2097176
  17.9 2.2 %collective-permute-done.2.refs_3_ = bf16[2,256,256]{2,1,0:T(8,128)(2,1)} collective-permute-done((bf16[2,256,256]{2,1,0:T(8,128)(2,1)S(1)}, bf16[2,256,256]{2,1,0:T(8,128)(2,1)}, u32[]{:S(2)}, u32[]{:S(2)}) %collective-permute-start.2) | collective-permute-done | bytes 262176 | tf_op jit(solution)/shard_map/ppermute | solution.py:190
  20.1 1.8 %shard_map.86.refs_1_.refs_0_ = bf16[2,256,256]{2,1,0:T(8,128)(2,1)S(1)} custom-call(bf16[4,512,512]{2,1,0:T(8,128)(2,1)S(1)} %shard_map.85.k_ref, bf16[2,256,256]{2,1,0:T(8,128)(2,1)S(1)} %bitcast_convert_fusion.refs_0_, bf16[2,256,256]{2,1,0:T(8,128)(2,1)S(1)} %collective-permute-done.refs_1_, bf16[2,256,256]{2,1,0:T(8,128)(2,1)} %collective-permute-done.1.refs_2_, ...), custom_call_target="tpu_custom_call" | custom-call | flops 536870912 | bytes 3145728 | tf_op jit(solution)/shard_map/pallas_call | solution.py:23
  23.3 1.3 %collective-permute-start.8 = (bf16[2,256,256]{2,1,0:T(8,128)(2,1)S(1)}, bf16[2,256,256]{2,1,0:T(8,128)(2,1)S(1)}, u32[]{:S(2)}, u32[]{:S(2)}) collective-permute-start(bf16[2,256,256]{2,1,0:T(8,128)(2,1)S(1)} %broadcast_select_fusion.1), channel_id=1, source_target_pairs={{4,6},{5,7},{2,0},{3,1},{12,14},{13,15},{10,8},{11,9},{20,22},{21,... | collective-permute-start | bytes 786440 | tf_op jit(solution)/shard_map/ppermute | solution.py:193
  24.6 4.6 %collective-permute-start.10 = (bf16[2,256,256]{2,1,0:T(8,128)(2,1)S(1)}, bf16[2,256,256]{2,1,0:T(8,128)(2,1)S(1)}, u32[]{:S(2)}, u32[]{:S(2)}) collective-permute-start(bf16[2,256,256]{2,1,0:T(8,128)(2,1)S(1)} %shard_map.86.refs_1_.refs_0_), channel_id=1, source_target_pairs={{16,0},{24,8},{0,16},{8,24},{17,1},{25,9},{1,17},{9,25},{18,2},{26... | collective-permute-start | bytes 786440 | tf_op jit(solution)/shard_map/ppermute | solution.py:190
  29.2 2.0 %collective-permute-start.11 = (bf16[2,256,256]{2,1,0:T(8,128)(2,1)S(1)}, bf16[2,256,256]{2,1,0:T(8,128)(2,1)S(1)}, u32[]{:S(2)}, u32[]{:S(2)}) collective-permute-start(bf16[2,256,256]{2,1,0:T(8,128)(2,1)S(1)} %shard_map.86.refs_1_.refs_0_), channel_id=1, source_target_pairs={{24,0},{16,8},{8,16},{0,24},{25,1},{17,9},{9,17},{1,25},{26,2},{18... | collective-permute-start | bytes 786440 | tf_op jit(solution)/shard_map/ppermute | solution.py:190
  31.4 17.9 %collective-permute-done.8.refs_5_ = bf16[2,256,256]{2,1,0:T(8,128)(2,1)S(1)} collective-permute-done((bf16[2,256,256]{2,1,0:T(8,128)(2,1)S(1)}, bf16[2,256,256]{2,1,0:T(8,128)(2,1)S(1)}, u32[]{:S(2)}, u32[]{:S(2)}) %collective-permute-start.8) | collective-permute-done | bytes 262176 | tf_op jit(solution)/shard_map/ppermute | solution.py:193
  61.0 1.2 shard_map.89.refs_4_
  62.2 1.9 %shard_map.90 = (f32[2,256,256]{2,1,0:T(8,128)S(1)}, bf16[2,256,256]{2,1,0:T(8,128)(2,1)S(1)}) custom-call(s32[5,8]{1,0:T(8,128)S(1)} %pad_add_fusion.meta, bf16[9,256,256]{2,1,0:T(8,128)(2,1)} %collective-permute-done.12.left_ref, bf16[2,256,256]{2,1,0:T(8,128)(2,1)S(1)} %copy-done.6, bf16[2,256,256]{2,1,0:T(8,128)(2,1)S(1)} %copy-done.17, ...), custom_call_target="tpu_custom_call" | custom-call | flops 268435456 | bytes 3145728 | tf_op jit(solution)/shard_map/pallas_call | solution.py:23
  64.9 1.3 %collective-permute-start.17 = (bf16[2,256,256]{2,1,0:T(8,128)(2,1)S(1)}, bf16[2,256,256]{2,1,0:T(8,128)(2,1)S(1)}, u32[]{:S(2)}, u32[]{:S(2)}) collective-permute-start(bf16[2,256,256]{2,1,0:T(8,128)(2,1)S(1)} %get-tuple-element.8.refs_0_), channel_id=1, source_target_pairs={{0,2},{1,3},{2,4},{3,5},{4,6},{5,7},{8,10},{9,11},{10,12},{11,13},... | collective-permute-start | bytes 786440 | tf_op jit(solution)/shard_map/ppermute | solution.py:193
  66.2 1.3 %collective-permute-start.18 = (bf16[2,256,256]{2,1,0:T(8,128)(2,1)S(1)}, bf16[2,256,256]{2,1,0:T(8,128)(2,1)S(1)}, u32[]{:S(2)}, u32[]{:S(2)}) collective-permute-start(bf16[2,256,256]{2,1,0:T(8,128)(2,1)S(1)} %get-tuple-element.8.refs_0_), channel_id=1, source_target_pairs={{2,0},{3,1},{4,2},{5,3},{6,4},{7,5},{10,8},{11,9},{12,10},{13,11},... | collective-permute-start | bytes 786440 | tf_op jit(solution)/shard_map/ppermute | solution.py:193
  67.6 2.6 %collective-permute-start.15 = (bf16[2,256,256]{2,1,0:T(8,128)(2,1)S(1)}, bf16[2,256,256]{2,1,0:T(8,128)(2,1)S(1)}, u32[]{:S(2)}, u32[]{:S(2)}) collective-permute-start(bf16[2,256,256]{2,1,0:T(8,128)(2,1)S(1)} %get-tuple-element.8.refs_0_), channel_id=1, source_target_pairs={{24,0},{16,8},{8,16},{0,24},{25,1},{17,9},{9,17},{1,25},{26,2},{18... | collective-permute-start | bytes 786440 | tf_op jit(solution)/shard_map/ppermute | solution.py:190
  70.2 1.7 %collective-permute-done.17.refs_1_ = bf16[2,256,256]{2,1,0:T(8,128)(2,1)S(1)} collective-permute-done((bf16[2,256,256]{2,1,0:T(8,128)(2,1)S(1)}, bf16[2,256,256]{2,1,0:T(8,128)(2,1)S(1)}, u32[]{:S(2)}, u32[]{:S(2)}) %collective-permute-start.17) | collective-permute-done | bytes 262176 | tf_op jit(solution)/shard_map/ppermute | solution.py:193
  72.6 3.2 %collective-permute-done.18.refs_2_ = bf16[2,256,256]{2,1,0:T(8,128)(2,1)S(1)} collective-permute-done((bf16[2,256,256]{2,1,0:T(8,128)(2,1)S(1)}, bf16[2,256,256]{2,1,0:T(8,128)(2,1)S(1)}, u32[]{:S(2)}, u32[]{:S(2)}) %collective-permute-start.18) | collective-permute-done | bytes 262176 | tf_op jit(solution)/shard_map/ppermute | solution.py:193
  75.8 1.3 %collective-permute-start.20 = (bf16[2,256,256]{2,1,0:T(8,128)(2,1)S(1)}, bf16[2,256,256]{2,1,0:T(8,128)(2,1)S(1)}, u32[]{:S(2)}, u32[]{:S(2)}) collective-permute-start(bf16[2,256,256]{2,1,0:T(8,128)(2,1)S(1)} %collective-permute-done.18.refs_2_), channel_id=1, source_target_pairs={{2,0},{3,1},{4,2},{5,3},{10,8},{11,9},{12,10},{13,11},{18,16},{19,... | collective-permute-start | bytes 786440 | tf_op jit(solution)/shard_map/ppermute | solution.py:193
  77.1 3.9 %collective-permute-done.14.refs_2_ = bf16[2,256,256]{2,1,0:T(8,128)(2,1)S(1)} collective-permute-done((bf16[2,256,256]{2,1,0:T(8,128)(2,1)S(1)}, bf16[2,256,256]{2,1,0:T(8,128)(2,1)S(1)}, u32[]{:S(2)}, u32[]{:S(2)}) %collective-permute-start.14) | collective-permute-done | bytes 262176 | tf_op jit(solution)/shard_map/ppermute | solution.py:190
  82.4 2.1 %collective-permute-done.20.refs_4_ = bf16[2,256,256]{2,1,0:T(8,128)(2,1)S(1)} collective-permute-done((bf16[2,256,256]{2,1,0:T(8,128)(2,1)S(1)}, bf16[2,256,256]{2,1,0:T(8,128)(2,1)S(1)}, u32[]{:S(2)}, u32[]{:S(2)}) %collective-permute-start.20) | collective-permute-done | bytes 262176 | tf_op jit(solution)/shard_map/ppermute | solution.py:193
  84.6 1.3 %collective-permute-start.21 = (bf16[2,256,256]{2,1,0:T(8,128)(2,1)S(1)}, bf16[2,256,256]{2,1,0:T(8,128)(2,1)S(1)}, u32[]{:S(2)}, u32[]{:S(2)}) collective-permute-start(bf16[2,256,256]{2,1,0:T(8,128)(2,1)S(1)} %broadcast_select_fusion), channel_id=1, source_target_pairs={{4,6},{5,7},{2,0},{3,1},{12,14},{13,15},{10,8},{11,9},{20,22},{21,... | collective-permute-start | bytes 786440 | tf_op jit(solution)/shard_map/ppermute | solution.py:193
  85.9 2.9 %collective-permute-start.22 = (bf16[2,256,256]{2,1,0:T(8,128)(2,1)S(1)}, bf16[2,256,256]{2,1,0:T(8,128)(2,1)S(1)}, u32[]{:S(2)}, u32[]{:S(2)}) collective-permute-start(bf16[2,256,256]{2,1,0:T(8,128)(2,1)S(1)} %shard_map.91.refs_1_.refs_0_), channel_id=1, source_target_pairs={{8,0},{0,8},{24,16},{16,24},{9,1},{1,9},{25,17},{17,25},{10,2},{2,... | collective-permute-start | bytes 786440 | tf_op jit(solution)/shard_map/ppermute | solution.py:190
  88.8 3.7 %collective-permute-start.23 = (bf16[2,256,256]{2,1,0:T(8,128)(2,1)S(1)}, bf16[2,256,256]{2,1,0:T(8,128)(2,1)S(1)}, u32[]{:S(2)}, u32[]{:S(2)}) collective-permute-start(bf16[2,256,256]{2,1,0:T(8,128)(2,1)S(1)} %shard_map.91.refs_1_.refs_0_), channel_id=1, source_target_pairs={{16,0},{24,8},{0,16},{8,24},{17,1},{25,9},{1,17},{9,25},{18,2},{26... | collective-permute-start | bytes 786440 | tf_op jit(solution)/shard_map/ppermute | solution.py:190
  92.5 16.0 %collective-permute-done.21.refs_5_ = bf16[2,256,256]{2,1,0:T(8,128)(2,1)S(1)} collective-permute-done((bf16[2,256,256]{2,1,0:T(8,128)(2,1)S(1)}, bf16[2,256,256]{2,1,0:T(8,128)(2,1)S(1)}, u32[]{:S(2)}, u32[]{:S(2)}) %collective-permute-start.21) | collective-permute-done | bytes 262176 | tf_op jit(solution)/shard_map/ppermute | solution.py:193
  111.9 1.9 %collective-permute-start.25 = (bf16[9,256,256]{2,1,0:T(8,128)(2,1)}, bf16[9,256,256]{2,1,0:T(8,128)(2,1)S(1)}, u32[]{:S(2)}, u32[]{:S(2)}) collective-permute-start(bf16[9,256,256]{2,1,0:T(8,128)(2,1)} %shard_map.93.left_ref), channel_id=1, source_target_pairs={{1,0},{0,1},{3,2},{2,3},{5,4},{4,5},{7,6},{6,7},{9,8},{8,9},{11,10... | collective-permute-start | bytes 3538952 | tf_op jit(solution)/shard_map/ppermute | solution.py:250
  113.7 1.3 %copy-done.4 = bf16[9,256,256]{2,1,0:T(8,128)(2,1)S(1)} copy-done((bf16[9,256,256]{2,1,0:T(8,128)(2,1)S(1)}, bf16[9,256,256]{2,1,0:T(8,128)(2,1)}, u32[]{:S(2)}) %copy-start.4) | copy-done | bytes 1179672
  118.8 1.2 shard_map.94.refs_4_
  120.1 2.0 %shard_map.95 = (f32[2,256,256]{2,1,0:T(8,128)}, bf16[2,256,256]{2,1,0:T(8,128)(2,1)}) custom-call(s32[5,8]{1,0:T(8,128)S(1)} %pad_add_fusion.meta, bf16[9,256,256]{2,1,0:T(8,128)(2,1)S(1)} %collective-permute-done.25.left_ref, bf16[2,256,256]{2,1,0:T(8,128)(2,1)S(1)} %copy-done.8, bf16[2,256,256]{2,1,0:T(8,128)(2,1)S(1)} %copy-done.20, ...), custom_call_target="tpu_custom_call" | custom-call | flops 268435456 | bytes 3145728 | tf_op jit(solution)/shard_map/pallas_call | solution.py:23
  (125 shorter events, 27.7 us)
Async XLA Ops:
  1.1 10.6 %collective-permute-start.4 = (bf16[2,256,256]{2,1,0:T(8,128)(2,1)S(1)}, bf16[2,256,256]{2,1,0:T(8,128)(2,1)S(1)}, u32[]{:S(2)}, u32[]{:S(2)}) collective-permute-start(bf16[2,256,256]{2,1,0:T(8,128)(2,1)S(1)} %bitcast_convert_fusion.refs_0_), channel_id=1, source_target_pairs={{0,2},{1,3},{2,4},{3,5},{4,6},{5,7},{8,10},{9,11},{10,12},{11,13},... | collective-permute-start | bytes 786440 | tf_op jit(solution)/shard_map/ppermute | solution.py:193
  5.1 8.9 %collective-permute-start.5 = (bf16[2,256,256]{2,1,0:T(8,128)(2,1)S(1)}, bf16[2,256,256]{2,1,0:T(8,128)(2,1)S(1)}, u32[]{:S(2)}, u32[]{:S(2)}) collective-permute-start(bf16[2,256,256]{2,1,0:T(8,128)(2,1)S(1)} %bitcast_convert_fusion.refs_0_), channel_id=1, source_target_pairs={{2,0},{3,1},{4,2},{5,3},{6,4},{7,5},{10,8},{11,9},{12,10},{13,11},... | collective-permute-start | bytes 786440 | tf_op jit(solution)/shard_map/ppermute | solution.py:193
  6.4 11.4 %collective-permute-start = (bf16[2,256,256]{2,1,0:T(8,128)(2,1)S(1)}, bf16[2,256,256]{2,1,0:T(8,128)(2,1)S(1)}, u32[]{:S(2)}, u32[]{:S(2)}) collective-permute-start(bf16[2,256,256]{2,1,0:T(8,128)(2,1)S(1)} %bitcast_convert_fusion.refs_0_), channel_id=1, source_target_pairs={{8,0},{0,8},{24,16},{16,24},{9,1},{1,9},{25,17},{17,25},{10,2},{2,... | collective-permute-start | bytes 786440 | tf_op jit(solution)/shard_map/ppermute | solution.py:190
  7.7 10.1 %collective-permute-start.1 = (bf16[2,256,256]{2,1,0:T(8,128)(2,1)S(1)}, bf16[2,256,256]{2,1,0:T(8,128)(2,1)}, u32[]{:S(2)}, u32[]{:S(2)}) collective-permute-start(bf16[2,256,256]{2,1,0:T(8,128)(2,1)S(1)} %bitcast_convert_fusion.refs_0_), channel_id=1, source_target_pairs={{16,0},{24,8},{0,16},{8,24},{17,1},{25,9},{1,17},{9,25},{18,2},{26... | collective-permute-start | bytes 786440 | tf_op jit(solution)/shard_map/ppermute | solution.py:190
  9.0 11.1 %collective-permute-start.2 = (bf16[2,256,256]{2,1,0:T(8,128)(2,1)S(1)}, bf16[2,256,256]{2,1,0:T(8,128)(2,1)}, u32[]{:S(2)}, u32[]{:S(2)}) collective-permute-start(bf16[2,256,256]{2,1,0:T(8,128)(2,1)S(1)} %bitcast_convert_fusion.refs_0_), channel_id=1, source_target_pairs={{24,0},{16,8},{8,16},{0,24},{25,1},{17,9},{9,17},{1,25},{26,2},{18... | collective-permute-start | bytes 786440 | tf_op jit(solution)/shard_map/ppermute | solution.py:190
  11.8 10.8 %collective-permute-start.6 = (bf16[2,256,256]{2,1,0:T(8,128)(2,1)S(1)}, bf16[2,256,256]{2,1,0:T(8,128)(2,1)S(1)}, u32[]{:S(2)}, u32[]{:S(2)}) collective-permute-start(bf16[2,256,256]{2,1,0:T(8,128)(2,1)S(1)} %collective-permute-done.4.refs_1_), channel_id=1, source_target_pairs={{2,4},{3,5},{4,6},{5,7},{10,12},{11,13},{12,14},{13,15},{18,20},{1... | collective-permute-start | bytes 786440 | tf_op jit(solution)/shard_map/ppermute | solution.py:193
  14.0 9.2 %collective-permute-start.7 = (bf16[2,256,256]{2,1,0:T(8,128)(2,1)S(1)}, bf16[2,256,256]{2,1,0:T(8,128)(2,1)S(1)}, u32[]{:S(2)}, u32[]{:S(2)}) collective-permute-start(bf16[2,256,256]{2,1,0:T(8,128)(2,1)S(1)} %collective-permute-done.5.refs_2_), channel_id=1, source_target_pairs={{2,0},{3,1},{4,2},{5,3},{10,8},{11,9},{12,10},{13,11},{18,16},{19,... | collective-permute-start | bytes 786440 | tf_op jit(solution)/shard_map/ppermute | solution.py:193
  17.8 31.4 %copy-start.33 = (bf16[2,256,256]{2,1,0:T(8,128)(2,1)S(1)}, bf16[2,256,256]{2,1,0:T(8,128)(2,1)}, u32[]{:S(2)}) copy-start(bf16[2,256,256]{2,1,0:T(8,128)(2,1)} %copy-done.32) | copy-start | bytes 786436
  17.8 31.4 %copy-start.35 = (bf16[2,256,256]{2,1,0:T(8,128)(2,1)S(1)}, bf16[2,256,256]{2,1,0:T(8,128)(2,1)}, u32[]{:S(2)}) copy-start(bf16[2,256,256]{2,1,0:T(8,128)(2,1)} %copy-done.34) | copy-start | bytes 786436
  21.8 28.1 %copy-start.5 = (bf16[2,256,256]{2,1,0:T(8,128)(2,1)}, bf16[2,256,256]{2,1,0:T(8,128)(2,1)S(1)}, u32[]{:S(2)}) copy-start(bf16[2,256,256]{2,1,0:T(8,128)(2,1)S(1)} %shard_map.86.refs_1_.refs_0_) | copy-start | bytes 786436
  21.9 9.5 %collective-permute-start.3 = (bf16[2,256,256]{2,1,0:T(8,128)(2,1)S(1)}, bf16[2,256,256]{2,1,0:T(8,128)(2,1)S(1)}, u32[]{:S(2)}, u32[]{:S(2)}) collective-permute-start(bf16[2,256,256]{2,1,0:T(8,128)(2,1)S(1)} %shard_map.86.refs_1_.refs_0_), channel_id=1, source_target_pairs={{0,0},{1,1},{2,8},{3,9},{4,16},{5,17},{6,24},{7,25},{8,2},{9,3},{1... | collective-permute-start | bytes 786440 | tf_op jit(solution)/shard_map/ppermute | solution.py:215
  23.3 26.0 %collective-permute-start.8 = (bf16[2,256,256]{2,1,0:T(8,128)(2,1)S(1)}, bf16[2,256,256]{2,1,0:T(8,128)(2,1)S(1)}, u32[]{:S(2)}, u32[]{:S(2)}) collective-permute-start(bf16[2,256,256]{2,1,0:T(8,128)(2,1)S(1)} %broadcast_select_fusion.1), channel_id=1, source_target_pairs={{4,6},{5,7},{2,0},{3,1},{12,14},{13,15},{10,8},{11,9},{20,22},{21,... | collective-permute-start | bytes 786440 | tf_op jit(solution)/shard_map/ppermute | solution.py:193
  24.6 26.5 %collective-permute-start.10 = (bf16[2,256,256]{2,1,0:T(8,128)(2,1)S(1)}, bf16[2,256,256]{2,1,0:T(8,128)(2,1)S(1)}, u32[]{:S(2)}, u32[]{:S(2)}) collective-permute-start(bf16[2,256,256]{2,1,0:T(8,128)(2,1)S(1)} %shard_map.86.refs_1_.refs_0_), channel_id=1, source_target_pairs={{16,0},{24,8},{0,16},{8,24},{17,1},{25,9},{1,17},{9,25},{18,2},{26... | collective-permute-start | bytes 786440 | tf_op jit(solution)/shard_map/ppermute | solution.py:190
  29.2 21.8 %collective-permute-start.11 = (bf16[2,256,256]{2,1,0:T(8,128)(2,1)S(1)}, bf16[2,256,256]{2,1,0:T(8,128)(2,1)S(1)}, u32[]{:S(2)}, u32[]{:S(2)}) collective-permute-start(bf16[2,256,256]{2,1,0:T(8,128)(2,1)S(1)} %shard_map.86.refs_1_.refs_0_), channel_id=1, source_target_pairs={{24,0},{16,8},{8,16},{0,24},{25,1},{17,9},{9,17},{1,25},{26,2},{18... | collective-permute-start | bytes 786440 | tf_op jit(solution)/shard_map/ppermute | solution.py:190
  31.2 19.9 %collective-permute-start.9 = (bf16[2,256,256]{2,1,0:T(8,128)(2,1)S(1)}, bf16[2,256,256]{2,1,0:T(8,128)(2,1)S(1)}, u32[]{:S(2)}, u32[]{:S(2)}) collective-permute-start(bf16[2,256,256]{2,1,0:T(8,128)(2,1)S(1)} %shard_map.86.refs_1_.refs_0_), channel_id=1, source_target_pairs={{8,0},{0,8},{24,16},{16,24},{9,1},{1,9},{25,17},{17,25},{10,2},{2,... | collective-permute-start | bytes 786440 | tf_op jit(solution)/shard_map/ppermute | solution.py:190
  31.4 18.6 %copy-start.26 = (bf16[2,256,256]{2,1,0:T(8,128)(2,1)}, bf16[2,256,256]{2,1,0:T(8,128)(2,1)S(1)}, u32[]{:S(2)}) copy-start(bf16[2,256,256]{2,1,0:T(8,128)(2,1)S(1)} %collective-permute-done.3.crossed_ref.refs_4_) | copy-start | bytes 786436
  52.5 9.7 %collective-permute-start.12 = (bf16[9,256,256]{2,1,0:T(8,128)(2,1)}, bf16[9,256,256]{2,1,0:T(8,128)(2,1)}, u32[]{:S(2)}, u32[]{:S(2)}) collective-permute-start(bf16[9,256,256]{2,1,0:T(8,128)(2,1)} %shard_map.88.left_ref), channel_id=1, source_target_pairs={{1,0},{0,1},{3,2},{2,3},{5,4},{4,5},{7,6},{6,7},{9,8},{8,9},{11,10... | collective-permute-start | bytes 3538952 | tf_op jit(solution)/shard_map/ppermute | solution.py:250
  64.9 7.0 %collective-permute-start.17 = (bf16[2,256,256]{2,1,0:T(8,128)(2,1)S(1)}, bf16[2,256,256]{2,1,0:T(8,128)(2,1)S(1)}, u32[]{:S(2)}, u32[]{:S(2)}) collective-permute-start(bf16[2,256,256]{2,1,0:T(8,128)(2,1)S(1)} %get-tuple-element.8.refs_0_), channel_id=1, source_target_pairs={{0,2},{1,3},{2,4},{3,5},{4,6},{5,7},{8,10},{9,11},{10,12},{11,13},... | collective-permute-start | bytes 786440 | tf_op jit(solution)/shard_map/ppermute | solution.py:193
  66.2 9.6 %collective-permute-start.18 = (bf16[2,256,256]{2,1,0:T(8,128)(2,1)S(1)}, bf16[2,256,256]{2,1,0:T(8,128)(2,1)S(1)}, u32[]{:S(2)}, u32[]{:S(2)}) collective-permute-start(bf16[2,256,256]{2,1,0:T(8,128)(2,1)S(1)} %get-tuple-element.8.refs_0_), channel_id=1, source_target_pairs={{2,0},{3,1},{4,2},{5,3},{6,4},{7,5},{10,8},{11,9},{12,10},{13,11},... | collective-permute-start | bytes 786440 | tf_op jit(solution)/shard_map/ppermute | solution.py:193
  67.5 9.6 %collective-permute-start.13 = (bf16[2,256,256]{2,1,0:T(8,128)(2,1)S(1)}, bf16[2,256,256]{2,1,0:T(8,128)(2,1)S(1)}, u32[]{:S(2)}, u32[]{:S(2)}) collective-permute-start(bf16[2,256,256]{2,1,0:T(8,128)(2,1)S(1)} %get-tuple-element.8.refs_0_), channel_id=1, source_target_pairs={{8,0},{0,8},{24,16},{16,24},{9,1},{1,9},{25,17},{17,25},{10,2},{2,... | collective-permute-start | bytes 786440 | tf_op jit(solution)/shard_map/ppermute | solution.py:190
  67.6 13.4 %collective-permute-start.14 = (bf16[2,256,256]{2,1,0:T(8,128)(2,1)S(1)}, bf16[2,256,256]{2,1,0:T(8,128)(2,1)S(1)}, u32[]{:S(2)}, u32[]{:S(2)}) collective-permute-start(bf16[2,256,256]{2,1,0:T(8,128)(2,1)S(1)} %get-tuple-element.8.refs_0_), channel_id=1, source_target_pairs={{16,0},{24,8},{0,16},{8,24},{17,1},{25,9},{1,17},{9,25},{18,2},{26... | collective-permute-start | bytes 786440 | tf_op jit(solution)/shard_map/ppermute | solution.py:190
  67.6 13.4 %collective-permute-start.15 = (bf16[2,256,256]{2,1,0:T(8,128)(2,1)S(1)}, bf16[2,256,256]{2,1,0:T(8,128)(2,1)S(1)}, u32[]{:S(2)}, u32[]{:S(2)}) collective-permute-start(bf16[2,256,256]{2,1,0:T(8,128)(2,1)S(1)} %get-tuple-element.8.refs_0_), channel_id=1, source_target_pairs={{24,0},{16,8},{8,16},{0,24},{25,1},{17,9},{9,17},{1,25},{26,2},{18... | collective-permute-start | bytes 786440 | tf_op jit(solution)/shard_map/ppermute | solution.py:190
  71.9 10.5 %collective-permute-start.19 = (bf16[2,256,256]{2,1,0:T(8,128)(2,1)S(1)}, bf16[2,256,256]{2,1,0:T(8,128)(2,1)S(1)}, u32[]{:S(2)}, u32[]{:S(2)}) collective-permute-start(bf16[2,256,256]{2,1,0:T(8,128)(2,1)S(1)} %collective-permute-done.17.refs_1_), channel_id=1, source_target_pairs={{2,4},{3,5},{4,6},{5,7},{10,12},{11,13},{12,14},{13,15},{18,20},{1... | collective-permute-start | bytes 786440 | tf_op jit(solution)/shard_map/ppermute | solution.py:193
  75.8 8.7 %collective-permute-start.20 = (bf16[2,256,256]{2,1,0:T(8,128)(2,1)S(1)}, bf16[2,256,256]{2,1,0:T(8,128)(2,1)S(1)}, u32[]{:S(2)}, u32[]{:S(2)}) collective-permute-start(bf16[2,256,256]{2,1,0:T(8,128)(2,1)S(1)} %collective-permute-done.18.refs_2_), channel_id=1, source_target_pairs={{2,0},{3,1},{4,2},{5,3},{10,8},{11,9},{12,10},{13,11},{18,16},{19,... | collective-permute-start | bytes 786440 | tf_op jit(solution)/shard_map/ppermute | solution.py:193
  81.7 27.5 %copy-start.7 = (bf16[2,256,256]{2,1,0:T(8,128)(2,1)}, bf16[2,256,256]{2,1,0:T(8,128)(2,1)S(1)}, u32[]{:S(2)}) copy-start(bf16[2,256,256]{2,1,0:T(8,128)(2,1)S(1)} %shard_map.91.refs_1_.refs_0_) | copy-start | bytes 786436
  81.7 10.8 %collective-permute-start.16 = (bf16[2,256,256]{2,1,0:T(8,128)(2,1)S(1)}, bf16[2,256,256]{2,1,0:T(8,128)(2,1)S(1)}, u32[]{:S(2)}, u32[]{:S(2)}) collective-permute-start(bf16[2,256,256]{2,1,0:T(8,128)(2,1)S(1)} %shard_map.91.refs_1_.refs_0_), channel_id=1, source_target_pairs={{0,0},{1,1},{2,8},{3,9},{4,16},{5,17},{6,24},{7,25},{8,2},{9,3},{1... | collective-permute-start | bytes 786440 | tf_op jit(solution)/shard_map/ppermute | solution.py:215
  84.6 23.9 %collective-permute-start.21 = (bf16[2,256,256]{2,1,0:T(8,128)(2,1)S(1)}, bf16[2,256,256]{2,1,0:T(8,128)(2,1)S(1)}, u32[]{:S(2)}, u32[]{:S(2)}) collective-permute-start(bf16[2,256,256]{2,1,0:T(8,128)(2,1)S(1)} %broadcast_select_fusion), channel_id=1, source_target_pairs={{4,6},{5,7},{2,0},{3,1},{12,14},{13,15},{10,8},{11,9},{20,22},{21,... | collective-permute-start | bytes 786440 | tf_op jit(solution)/shard_map/ppermute | solution.py:193
  85.9 24.5 %collective-permute-start.22 = (bf16[2,256,256]{2,1,0:T(8,128)(2,1)S(1)}, bf16[2,256,256]{2,1,0:T(8,128)(2,1)S(1)}, u32[]{:S(2)}, u32[]{:S(2)}) collective-permute-start(bf16[2,256,256]{2,1,0:T(8,128)(2,1)S(1)} %shard_map.91.refs_1_.refs_0_), channel_id=1, source_target_pairs={{8,0},{0,8},{24,16},{16,24},{9,1},{1,9},{25,17},{17,25},{10,2},{2,... | collective-permute-start | bytes 786440 | tf_op jit(solution)/shard_map/ppermute | solution.py:190
  88.8 21.5 %collective-permute-start.23 = (bf16[2,256,256]{2,1,0:T(8,128)(2,1)S(1)}, bf16[2,256,256]{2,1,0:T(8,128)(2,1)S(1)}, u32[]{:S(2)}, u32[]{:S(2)}) collective-permute-start(bf16[2,256,256]{2,1,0:T(8,128)(2,1)S(1)} %shard_map.91.refs_1_.refs_0_), channel_id=1, source_target_pairs={{16,0},{24,8},{0,16},{8,24},{17,1},{25,9},{1,17},{9,25},{18,2},{26... | collective-permute-start | bytes 786440 | tf_op jit(solution)/shard_map/ppermute | solution.py:190
  92.5 17.9 %collective-permute-start.24 = (bf16[2,256,256]{2,1,0:T(8,128)(2,1)S(1)}, bf16[2,256,256]{2,1,0:T(8,128)(2,1)S(1)}, u32[]{:S(2)}, u32[]{:S(2)}) collective-permute-start(bf16[2,256,256]{2,1,0:T(8,128)(2,1)S(1)} %shard_map.91.refs_1_.refs_0_), channel_id=1, source_target_pairs={{24,0},{16,8},{8,16},{0,24},{25,1},{17,9},{9,17},{1,25},{26,2},{18... | collective-permute-start | bytes 786440 | tf_op jit(solution)/shard_map/ppermute | solution.py:190
  92.5 16.8 %copy-start.28 = (bf16[2,256,256]{2,1,0:T(8,128)(2,1)}, bf16[2,256,256]{2,1,0:T(8,128)(2,1)S(1)}, u32[]{:S(2)}) copy-start(bf16[2,256,256]{2,1,0:T(8,128)(2,1)S(1)} %collective-permute-done.16.crossed_ref.refs_4_) | copy-start | bytes 786436
  111.9 8.2 %collective-permute-start.25 = (bf16[9,256,256]{2,1,0:T(8,128)(2,1)}, bf16[9,256,256]{2,1,0:T(8,128)(2,1)S(1)}, u32[]{:S(2)}, u32[]{:S(2)}) collective-permute-start(bf16[9,256,256]{2,1,0:T(8,128)(2,1)} %shard_map.93.left_ref), channel_id=1, source_target_pairs={{1,0},{0,1},{3,2},{2,3},{5,4},{4,5},{7,6},{6,7},{9,8},{8,9},{11,10... | collective-permute-start | bytes 3538952 | tf_op jit(solution)/shard_map/ppermute | solution.py:250
  (32 other events, 62.3 us)
